TPU v7x, 256 devices: a whole 4x4x8 slice. The times are simulated.
256 devices in a mesh: samples: 64 (over z, y, x_hi), params: 4 (over x_lo, core).
Axes of the slice: x: 4 (x_hi: 2, x_lo: 2; x = x_hi * 2 + x_lo), y: 4, z: 8, core: 2. Of those that a mesh axis runs over, the one named last changes fastest.
Arguments:
- occupations: int32 [4096, 152], P('samples'), may hold values from 0 to 1, as said below
- connection_counts: int32 [4096], P('samples'), may hold values from 0 to 3072, as said below
- connection_orbitals: int32 [4, 196608], P(None, ('samples', 'params')), may hold values from 0 to 151, as said below
- connection_elements: float32 [2, 196608], P(None, ('samples', 'params')), may hold values from -2 to 2
- laser_step: int32 [], replicated, may hold values from 0 to 3999
- first_weight: bfloat16 [152, 1024], replicated, may hold values from -4 to 4
- first_bias: float32 [1024], replicated, may hold values from -3 to 3
- second_weight: bfloat16 [1024, 256], P('params'), may hold values from -1.25 to 1.25
- readout: float32 [2, 256], replicated, may hold values from -0.375 to 0.375
Outputs:
- local_energy: float32 [2, 4096], P(None, 'samples')
- change: float32 [2, 4096], P(None, 'samples')
Inputs may be any that keep to these rules, and one draw needn't show every extreme that they name: `occupations`: each row has exactly 76 ones. `connection_counts`: the connections of block b of 64 consecutive samples fill the first slots q of that block in order of sample; the counts of a block sum to at most 3072, and to exactly 3072 in some block. `connection_orbitals`: the 4 orbitals of a slot are distinct; unused slots hold arbitrary orbitals in the range.
All inputs are finite; a program needn't handle non-finite values.
Results may differ from a plain program's by a relative error of at most 0.0099.
Values may be sent and summed in bfloat16 or wider, within the bound.
A program may use at most 64 MiB of HBM per device.

v0:
```python
import jax
import jax.numpy as jnp
from jax import lax
from jax.sharding import PartitionSpec as P

ITERS = 2


PRECISE = lax.Precision.HIGHEST
FIELD_SCALE = 0.8
FIELD_RATE = 0.0123
DIAG_SHIFT = 0.01
BLOCK_ROWS = 128


def slot_values(base_pre, orbitals, deltas, first_weight, full_second, readout):
    columns = jnp.arange(first_weight.shape[0], dtype=jnp.int32)
    flips = jnp.sum(
        deltas[:, :, None] * (orbitals[:, :, None] == columns[None, None, :]).astype(jnp.float32),
        axis=0,
    )
    slot_pre = base_pre + jnp.dot(
        flips.astype(jnp.bfloat16), first_weight, preferred_element_type=jnp.float32
    )
    slot_hidden = jnp.tanh(slot_pre).astype(jnp.bfloat16)
    slot_mid = jnp.tanh(jnp.dot(slot_hidden, full_second, preferred_element_type=jnp.float32))
    return jnp.dot(slot_mid, readout.T, precision=PRECISE)


def evaluate_slots(
    low_row,
    high_row,
    parent_pre,
    parent_logs,
    orbitals,
    deltas,
    parents,
    first_weight,
    full_second,
    readout,
):
    width = parents.shape[0]

    def one_block(block, ratios):
        start = block * BLOCK_ROWS
        parent_block = lax.dynamic_slice_in_dim(parents, start, BLOCK_ROWS)
        orbital_block = lax.dynamic_slice_in_dim(orbitals, start, BLOCK_ROWS, 1)
        delta_block = lax.dynamic_slice_in_dim(deltas, start, BLOCK_ROWS, 1)
        base_pre = jnp.take(parent_pre, parent_block, axis=0)
        slot_logs = slot_values(
            base_pre, orbital_block, delta_block, first_weight, full_second, readout
        )
        diff = slot_logs - jnp.take(parent_logs, parent_block, axis=0)
        magnitude = jnp.exp(diff[:, 0])
        piece = jnp.stack([magnitude * jnp.cos(diff[:, 1]), magnitude * jnp.sin(diff[:, 1])])
        return lax.dynamic_update_slice_in_dim(ratios, piece, start, 1)

    first_block = low_row // BLOCK_ROWS
    last_block = (high_row + BLOCK_ROWS - 1) // BLOCK_ROWS
    return lax.fori_loop(first_block, last_block, one_block, jnp.zeros((2, width), jnp.float32))


def body(
    occupations,
    connection_counts,
    connection_orbitals,
    connection_elements,
    laser_step,
    first_weight,
    first_bias,
    second_weight,
    readout,
):
    samples_here = occupations.shape[0]
    slots = connection_orbitals.shape[1]
    place = lax.axis_index("params")
    spread = lax.axis_size("params")
    field = FIELD_SCALE * jnp.sin(FIELD_RATE * laser_step.astype(jnp.float32))
    full_second = lax.all_gather(second_weight, "params", axis=0, tiled=True)
    pre = (
        jnp.dot(occupations.astype(jnp.bfloat16), first_weight, preferred_element_type=jnp.float32)
        + first_bias
    )
    hidden = jnp.tanh(pre).astype(jnp.bfloat16)
    mid = jnp.tanh(jnp.dot(hidden, full_second, preferred_element_type=jnp.float32))
    logs = jnp.dot(mid, readout.T, precision=PRECISE)
    cumulative = jnp.cumsum(connection_counts, dtype=jnp.int32)
    positions = place + spread * jnp.arange(slots, dtype=jnp.int32)
    parents = jnp.sum(
        (cumulative[None, :] <= positions[:, None]).astype(jnp.int32), axis=1, dtype=jnp.int32
    )
    parents = jnp.minimum(parents, samples_here - 1)
    used = positions < cumulative[-1]
    live_count = jnp.clip((cumulative[-1] - place + spread - 1) // spread, 0, slots)
    picked = jnp.take_along_axis(
        jnp.take(occupations, parents, axis=0), connection_orbitals.T, axis=1
    ).T
    deltas = 1.0 - 2.0 * picked.astype(jnp.float32)
    ratio = evaluate_slots(
        0,
        live_count,
        pre,
        logs,
        connection_orbitals,
        deltas,
        parents,
        first_weight,
        full_second,
        readout,
    )
    weight = connection_elements[0] + field * connection_elements[1]
    contrib = jnp.where(used[None, :], weight[None, :] * ratio, 0.0)
    owners = jnp.arange(samples_here, dtype=jnp.int32)
    select = ((parents[None, :] == owners[:, None]) & used[None, :]).astype(jnp.float32)
    partial_energy = jnp.dot(contrib, select.T, precision=PRECISE)
    local_energy = lax.psum(partial_energy, "params")
    width = second_weight.shape[0]
    hidden_part = lax.dynamic_slice_in_dim(hidden, place * width, width, 1).astype(jnp.float32)
    slope = 1.0 - mid * mid
    slope_re = slope * readout[0]
    slope_im = slope * readout[1]
    sample_total = float(samples_here * lax.axis_size("samples"))
    energy_sum = lax.psum(jnp.sum(local_energy, axis=1), "samples")
    emean = energy_sum / sample_total
    centered = local_energy - emean[:, None]
    weighted = slope_re * centered[1][:, None] - slope_im * centered[0][:, None]
    sum_re, sum_im, sum_force = lax.psum(
        (
            jnp.dot(hidden_part.T, slope_re, precision=PRECISE),
            jnp.dot(hidden_part.T, slope_im, precision=PRECISE),
            jnp.dot(hidden_part.T, weighted, precision=PRECISE),
        ),
        "samples",
    )
    obar_re = sum_re / sample_total
    obar_im = sum_im / sample_total
    force = sum_force / sample_total

    def project(vector):
        lifted = jnp.dot(hidden_part, vector, precision=PRECISE)
        raw = jnp.stack([jnp.sum(lifted * slope_re, axis=1), jnp.sum(lifted * slope_im, axis=1)])
        means = jnp.stack([jnp.sum(obar_re * vector), jnp.sum(obar_im * vector)])
        raw_total, mean_total = lax.psum((raw, means), "params")
        return raw_total - mean_total[:, None]

    def squared(vector):
        return lax.psum(jnp.sum(vector * vector), "params")

    solution = jnp.zeros_like(force)
    residual = force
    direction = force
    norm_now = squared(residual)
    for turn in range(ITERS):
        coeffs = project(direction)
        back = slope_re * coeffs[0][:, None] + slope_im * coeffs[1][:, None]
        summed = lax.psum(jnp.dot(hidden_part.T, back, precision=PRECISE), "samples")
        image = summed / sample_total + DIAG_SHIFT * direction
        curv = lax.psum(jnp.sum(direction * image), "params")
        alpha = norm_now / curv
        solution = solution + alpha * direction
        residual = residual - alpha * image
        if turn + 1 < ITERS:
            norm_next = squared(residual)
            direction = residual + norm_next / norm_now * direction
            norm_now = norm_next
    change = project(solution)
    return (local_energy, change)


def solution(mesh):
    return jax.shard_map(
        body,
        mesh=mesh,
        in_specs=(
            P("samples", None),
            P("samples"),
            P(None, ("samples", "params")),
            P(None, ("samples", "params")),
            P(),
            P(),
            P(),
            P("params", None),
            P(),
        ),
        out_specs=(P(None, "samples"), P(None, "samples")),
        check_vma=False,
    )
```

profile of v0, /device:TPU:1, one launch (start us, length us, event | category | flops | bytes accessed | tf_op | source)
XLA Modules:
  0.0 2264.7 jit_solution(1647701345181177747)
XLA Ops:
  7.2 0.7 copy.37
  8.2 0.5 slice.61
  8.7 0.7 broadcast_compare_fusion
  10.2 0.7 fusion.42
  10.9 0.2 copy.38
  11.1 0.2 reshape.147
  11.3 2.1 gather_fusion.2
  13.5 0.2 broadcast_select_fusion
  13.6 24.7 %gather_fusion.3 = s32[3072]{0:T(1024)S(1)} fusion(s32[768,152]{1,0:T(8,128)S(1)} %broadcast_select_fusion, s32[3072]{0:T(1024)S(1)} %reshape.147), kind=kCustom, calls=%fused_computation.3 | custom fusion | bytes 49152 | tf_op jit(solution)/shard_map/jit(take_along_axis)/gather | solution.py:95
  38.4 0.4 reshape.150
  38.8 0.1 copy.39
  39.1 0.2 copy-done.6
  39.3 9.6 all_gather.3
  48.9 0.2 tanh_convert_fusion
  49.1 0.2 convolution_tanh_fusion
  49.3 0.3 copy-done.7
  49.5 0.2 fusion.83
  49.7 9.9 while.10
  49.9 0.8 gather_fusion
  50.7 0.5 fusion.107
  51.2 0.6 gather_fusion.1
  51.9 0.2 convolution_subtract_fusion.2
  52.3 0.8 gather_fusion
  53.2 0.5 fusion.107
  53.7 0.6 gather_fusion.1
  54.4 0.2 convolution_subtract_fusion.2
  54.8 0.8 gather_fusion
  55.7 0.5 fusion.107
  56.2 0.6 gather_fusion.1
  56.9 0.2 convolution_subtract_fusion.2
  57.3 0.8 gather_fusion
  58.2 0.5 fusion.107
  58.6 0.6 gather_fusion.1
  59.4 0.2 convolution_subtract_fusion.2
  60.4 0.1 fusion.11
  60.6 5.2 psum.119
  65.9 155.5 %psum.120 = f32[2]{0:T(128)S(1)} all-reduce(f32[2]{0:T(128)S(1)} %reduce_sum.172), channel_id=1, replica_groups=mesh['samples'=64,'params'=4] {'samples'}, use_global_device_ids=true, to_apply=%region_7.8 | all-reduce | flops 2 | bytes 16 | tf_op jit(solution)/shard_map/psum | solution.py:123
  221.5 1.0 fusion.57
  222.6 1.0 fusion.55
  223.6 1.1 fusion.26
  224.7 658.2 %all-reduce.13.cloned.1.call-done = (f32[256,256]{1,0:T(8,128)}, f32[256,256]{1,0:T(8,128)}, f32[256,256]{1,0:T(8,128)}) async-done(((f32[256,256]{1,0:T(8,128)}, f32[256,256]{1,0:T(8,128)}, f32[256,256]{1,0:T(8,128)}), (f32[256,256]{1,0:T(8,128)}, f32[256,256]{1,0:T(8,128)}, f32[256,256]{1,0:T(8,128)})) %all-reduce.13.cloned.1.call-update) | async-done | bytes 786448 | tf_op jit(solution)/shard_map/psum | solution.py:127
  883.0 1.3 multiply_reduce_fusion.15
  884.3 1.9 multiply_reduce_fusion.8
  886.2 1.4 pad_maximum_fusion.3
  887.5 43.4 %all-reduce.4 = (f32[2,64]{1,0:T(2,128)S(1)}, f32[2]{0:T(128)S(1)}) all-reduce(f32[2,64]{1,0:T(2,128)S(1)} %pad_maximum_fusion, f32[2]{0:T(128)S(1)} %pad_maximum_fusion.3), channel_id=1, replica_groups=mesh['samples'=64,'params'=4] {'params'}, use_global_device_ids=true, to_apply=%region_13.14 | all-reduce | flops 130 | bytes 1040 | tf_op jit(solution)/shard_map/psum | solution.py:143
  931.0 1.1 fusion.22
  932.1 612.0 %all-reduce.9.cloned.1.call-done = f32[256,256]{1,0:T(8,128)} async-done(((f32[256,256]{1,0:T(8,128)}), f32[256,256]{1,0:T(8,128)}) %all-reduce.9.cloned.1.call-update) | async-done | bytes 262160 | tf_op jit(solution)/shard_map/psum | solution.py:156
  1544.2 1.8 multiply_reduce_fusion.6
  1545.9 34.5 %all-reduce.3 = (f32[]{:T(128)}, f32[]{:T(128)}) all-reduce(f32[]{:T(128)} %get-tuple-element.88, f32[]{:T(128)} %get-tuple-element.87), channel_id=1, replica_groups=mesh['samples'=64,'params'=4] {'params'}, use_global_device_ids=true, to_apply=%region_10.11 | all-reduce | flops 2 | bytes 16 | tf_op jit(solution)/shard_map/psum | solution.py:147
  1581.7 1.6 multiply_reduce_fusion.5
  1583.4 6.6 psum.129
  1591.2 0.8 multiply_reduce_fusion.4
  1592.0 0.3 multiply_reduce_fusion.13
  1592.3 1.3 pad_maximum_fusion.4
  1593.6 5.7 all-reduce.2
  1599.5 1.0 fusion.18
  1600.5 611.0 %all-reduce.11.cloned.1.call-done = f32[256,256]{1,0:T(8,128)} async-done(((f32[256,256]{1,0:T(8,128)}), f32[256,256]{1,0:T(8,128)}) %all-reduce.11.cloned.1.call-update) | async-done | bytes 262160 | tf_op jit(solution)/shard_map/psum | solution.py:156
  2211.5 1.7 multiply_reduce_fusion.2
  2213.2 34.6 %psum.133 = f32[]{:T(128)} all-reduce(f32[]{:T(128)} %multiply_reduce_fusion.2), channel_id=1, replica_groups=mesh['samples'=64,'params'=4] {'params'}, use_global_device_ids=true, to_apply=%region_32.33 | all-reduce | flops 1 | bytes 8 | tf_op jit(solution)/shard_map/psum | solution.py:158
  2249.1 0.8 multiply_reduce_fusion.1
  2249.9 0.3 multiply_reduce_fusion.11
  2250.2 1.4 pad_maximum_fusion.5
  2251.6 5.9 all-reduce.1
  2257.6 0.6 broadcast_subtract_fusion
  (83 shorter events, 2.4 us)
Async XLA Ops:
  7.2 4.2 copy-start
  7.2 875.8 %all-reduce.13.cloned.1.call-start = ((), (), s32[]{:S(2)}) async-start(), calls=%async_computation.2 | async-start | bytes 1572864 | tf_op jit(solution)/shard_map/psum | solution.py:127
  38.4 0.7 copy-start.8
  38.4 0.9 copy-start.6
  38.4 10.5 copy-start.1
  38.4 10.5 copy-start.11
  48.9 0.7 copy-start.7
  49.7 10.7 copy-start.10
  65.8 158.9 %copy-start.9 = (f32[2,64]{1,0:T(2,128)}, f32[2,64]{1,0:T(2,128)S(1)}, u32[]{:S(2)}) copy-start(f32[2,64]{1,0:T(2,128)S(1)} %psum.119) | copy-start | bytes 1540
  224.7 1319.4 %all-reduce.9.cloned.1.call-start = ((), (), s32[]{:S(2)}) async-start(), calls=%async_computation | async-start | bytes 524288 | tf_op jit(solution)/shard_map/psum | solution.py:156
  884.3 659.9 %copy-start.2 = (f32[256,256]{1,0:T(8,128)S(1)}, f32[256,256]{1,0:T(8,128)}, u32[]{:S(2)}) copy-start(f32[256,256]{1,0:T(8,128)} %get-tuple-element.119) | copy-start | bytes 786436
  931.0 660.2 %copy-start.3 = (f32[256,256]{1,0:T(8,128)S(1)}, f32[256,256]{1,0:T(8,128)}, u32[]{:S(2)}) copy-start(f32[256,256]{1,0:T(8,128)} %get-tuple-element.120) | copy-start | bytes 786436
  931.0 660.2 %copy-start.4 = (f32[256,256]{1,0:T(8,128)S(1)}, f32[256,256]{1,0:T(8,128)}, u32[]{:S(2)}) copy-start(f32[256,256]{1,0:T(8,128)} %get-tuple-element.121) | copy-start | bytes 786436
  932.1 1279.4 %all-reduce.11.cloned.1.call-start = ((), (), s32[]{:S(2)}) async-start(), calls=%async_computation.1 | async-start | bytes 524288 | tf_op jit(solution)/shard_map/psum | solution.py:156
  1544.2 47.0 %copy-start.5 = (f32[256,256]{1,0:T(8,128)S(1)}, f32[256,256]{1,0:T(8,128)}, u32[]{:S(2)}) copy-start(f32[256,256]{1,0:T(8,128)} %all-reduce.9.cloned.1.call-done) | copy-start | bytes 786436
Sparse Core Ops, SparseCore 0:
  224.8 658.1 all-reduce.12
  932.2 611.8 all-reduce.8
  1600.6 610.7 all-reduce.10
where the time goes:
time: 2270 us; the launch traced here: 2260 us
  waiting for transfers between devices  1880 us (83%)
  blocking collectives  301 us (13%)
  local copies, waits for them, and re-layouts  35.8 us (2%)
    psum x2, waiting for transfers between devices, body(): lax.psum(jnp.dot(hidden_part.T, back, precision=PRECISE), 'samples')  1220 us
    psum x1, waiting for transfers between devices, body(): lax.psum((jnp.dot(hidden_part.T, slope_re, precision=PRECISE), jnp.dot(hi...  658 us
    psum x1, blocking collectives, body(): energy_sum = lax.psum(jnp.sum(local_energy, axis=1), 'samples')  156 us
    psum x3, blocking collectives, project(): raw_total, mean_total = lax.psum((raw, means), 'params')  55.1 us
  transfers between devices with their start and end apart: 3, of which 3 were waited for; matrix products, arithmetic and copies ran while one was open for 0% of the time, Pallas kernels for 0%

commit v1 on v0

v1 whole, which is shorter than its diff:
```python
import functools

import jax
import jax.numpy as jnp
from jax import lax
from jax.experimental import pallas as pl
from jax.experimental.pallas import tpu as pltpu
from jax.sharding import PartitionSpec as P

FIELD_SCALE = 0.8
FIELD_RATE = 0.0123
DIAG_SHIFT = 0.01
MESH = pl.DeviceIdType.MESH
F32 = jnp.float32
BF16 = jnp.bfloat16


def sincos(x):
    n = jnp.floor(x * 0.6366197723675814 + 0.5)
    r = x - n * 1.5703125
    r = r - n * 4.8351287841796875e-4
    r = r - n * 3.1385570764541626e-7
    r = r - n * 6.0771005065061922e-11
    z = r * r
    s = r + r * z * (-1.6666654611e-1 + z * (8.3321608736e-3 - z * 1.9515295891e-4))
    c = 1.0 - 0.5 * z + z * z * (
        4.166664568298827e-2 + z * (-1.388731625493765e-3 + z * 2.443315711809948e-5)
    )
    quad = n - 4.0 * jnp.floor(n * 0.25)
    odd = (quad == 1.0) | (quad == 3.0)
    sin = jnp.where(odd, c, s)
    cos = jnp.where(odd, s, c)
    sin = jnp.where(quad >= 2.0, -sin, sin)
    cos = jnp.where((quad == 1.0) | (quad == 2.0), -cos, cos)
    return sin, cos


def parts3(x):
    hi = x.astype(BF16).astype(F32)
    rest = x - hi
    mid = rest.astype(BF16).astype(F32)
    return hi, mid, rest - mid


def pack_rows(rows, height):
    width = rows[0].shape[1]
    place = lax.broadcasted_iota(jnp.int32, (height, width), 0)
    out = jnp.zeros((height, width), F32)
    for i, row in enumerate(rows):
        out = jnp.where(place == i, jnp.broadcast_to(row, (height, width)), out)
    return out


def nn(a, b):
    return lax.dot_general(a, b, (((1,), (0,)), ((), ())), preferred_element_type=F32)


def nt(a, b):
    return lax.dot_general(a, b, (((1,), (1,)), ((), ())), preferred_element_type=F32)


def tn(a, b):
    return lax.dot_general(a, b, (((0,), (0,)), ((), ())), preferred_element_type=F32)


def kernel(
    n_params,
    n_groups,
    occ_ref,
    counts_ref,
    orb_ref,
    elem_ref,
    step_ref,
    w1_ref,
    bias_ref,
    w2_ref,
    readout_ref,
    out_ref,
    occ_mine,
    occ_col,
    occ_row,
    w2_full,
    slot_hid,
    pick,
    kt_hi,
    kt_lo,
    e_msg,
    e_buf,
    y_msg,
    y_buf,
    z_msg,
    z_buf,
    s_msg,
    s_buf,
    change_buf,
    w2_send,
    w2_recv,
    col_send,
    col_recv,
    row_send,
    row_recv,
    e_send,
    e_recv,
    y_send,
    y_recv,
    z_send,
    z_recv,
    s_send,
    s_recv,
):
    samples, orbitals = occ_ref.shape
    slots = orb_ref.shape[1]
    depth = w2_ref.shape[0]
    hid2 = w2_ref.shape[1]
    pn = n_params
    cn = n_groups
    g = cn // pn
    block = g * samples
    total = float(block * cn)

    b = lax.axis_index("samples")
    p = lax.axis_index("params")
    k = b // g
    q = b % g
    l = q * pn + p
    alone = l == k

    def member(group, m):
        return (group * g + m // pn, m % pn)

    barrier = pltpu.get_barrier_semaphore()

    def signal(device):
        pl.semaphore_signal(barrier, inc=1, device_id=device, device_id_type=MESH)

    def greet(d, carry):
        signal(member(k, lax.rem(l + d, cn)))
        j = lax.rem(k + d, cn)
        signal((j * g + k // pn, k % pn))
        return carry

    lax.fori_loop(1, cn, greet, 0)

    @pl.when(jnp.logical_not(alone))
    def _():
        signal((k * g + k // pn, k % pn))

    for i in range(g):

        @pl.when(jnp.logical_not(alone & (q == i)))
        def _():
            signal((l * g + i, k % pn))

    occ = occ_ref[...].astype(F32)
    occ_mine[...] = jnp.zeros_like(occ_mine)
    occ_mine[:, :orbitals] = occ.astype(BF16)

    pl.semaphore_wait(barrier, jnp.where(alone, 2 * cn + g - 3, 2 * cn + g - 1))

    half = depth // 2
    copies = []

    def start(src, dst, send, recv, device):
        copy = pltpu.make_async_remote_copy(
            src_ref=src, dst_ref=dst, send_sem=send, recv_sem=recv, device_id=device, device_id_type=MESH
        )
        copy.start()
        return copy

    p_core = p + 1 - 2 * (p % 2)
    b_pair = b + 1 - 2 * (b % 2)
    whole = pl.ds(pl.multiple_of(p * depth, depth), depth)
    copies.append(start(w2_ref, w2_full.at[whole], w2_send.at[0], w2_recv.at[0], (b, p_core)))
    if pn == 4:
        for d in (0, 1):
            far = (p // 2) * (-2) + 2 + (p % 2 + d) % 2
            for h, to in ((0, b), (1, b_pair)):
                rows = pl.ds(pl.multiple_of(p * depth + h * half, half), half)
                i = 1 + d * 2 + h
                copies.append(
                    start(w2_ref.at[pl.ds(h * half, half)], w2_full.at[rows], w2_send.at[i], w2_recv.at[i], (to, far))
                )
    for d in range(1, g):
        i = lax.rem(q + d, g)
        copies.append(start(occ_mine, occ_col.at[q], col_send.at[d], col_recv.at[g - d], (k * g + i, p)))

    def row_copy(t):
        kk = p + pn * t
        return pltpu.make_async_remote_copy(
            src_ref=occ_mine,
            dst_ref=occ_row.at[q],
            send_sem=row_send.at[t],
            recv_sem=row_recv.at[q],
            device_id=(kk * g + k // pn, k % pn),
            device_id_type=MESH,
        )

    for t in range(cn // pn):

        @pl.when(jnp.logical_not(alone & (k == p + pn * t)))
        def _():
            row_copy(t).start()

    w2_full[whole] = w2_ref[...]
    occ_col[q] = occ_mine[...]

    @pl.when(alone)
    def _():
        occ_row[q] = occ_mine[...]

    counts = jnp.broadcast_to(counts_ref[...].astype(F32), (8, samples))
    r_id = lax.broadcasted_iota(jnp.int32, (samples, samples), 0)
    c_id = lax.broadcasted_iota(jnp.int32, (samples, samples), 1)
    upto = (r_id <= c_id).astype(BF16)
    c_hi, c_mid, c_lo = parts3(counts)
    ends = nn(c_hi.astype(BF16), upto) + nn(c_mid.astype(BF16), upto) + nn(c_lo.astype(BF16), upto)
    begins = ends - counts
    ends, begins = ends[0:1], begins[0:1]
    position = (p + pn * lax.broadcasted_iota(jnp.int32, (slots, samples), 0)).astype(F32)
    pick[...] = ((begins <= position) & (position < ends)).astype(BF16)
    occ_t = occ.T.astype(BF16)
    w1 = w1_ref[...]
    bias = bias_ref[...]
    chunk = 256
    for start_row in range(0, slots, chunk):
        rows = slice(start_row, start_row + chunk)
        base = nt(occ_t, pick[rows])
        column = lax.broadcasted_iota(jnp.int32, (orbitals, chunk), 0)
        orb = orb_ref[:, rows]
        flip = orb[0:1] == column
        for u in range(1, orb_ref.shape[0]):
            flip = flip | (orb[u : u + 1] == column)
        flipped = jnp.where(flip, 1.0 - base, base).astype(BF16)
        slot_hid[rows] = jnp.tanh(tn(flipped, w1) + bias).astype(BF16)
    hidden = jnp.tanh(nn(occ_mine[:, :orbitals], w1) + bias).astype(BF16)

    for copy in copies[: 5 if pn == 4 else 1]:
        copy.wait_recv()
    w2 = w2_full[...]

    readout = readout_ref[...]
    r_rows = pack_rows([x[i : i + 1] for x in parts3(readout) for i in range(2)], 16).astype(BF16)

    def logs_of(hid):
        mid = jnp.tanh(nn(hid, w2))
        hi = mid.astype(BF16)
        lo = (mid - hi.astype(F32)).astype(BF16)
        out = nt(r_rows, hi) + nt(r_rows, lo)
        return out[0:2] + out[2:4] + out[4:6]

    logs = logs_of(hidden)
    slot_logs = logs_of(slot_hid[...])
    l_rows = pack_rows([x[i : i + 1] for x in parts3(logs) for i in range(2)], 16).astype(BF16)
    parent_logs = nt(l_rows, pick[...])
    parent_logs = parent_logs[0:2] + parent_logs[2:4] + parent_logs[4:6]
    diff = slot_logs - parent_logs
    angle = jnp.full((1, slots), step_ref[0, 0], jnp.int32).astype(F32) * FIELD_RATE
    field = FIELD_SCALE * sincos(angle)[0]
    elem = elem_ref[...]
    weight = elem[0:1] + field * elem[1:2]
    slot_at = (p + pn * lax.broadcasted_iota(jnp.int32, (1, slots), 1)).astype(F32)
    used = slot_at < ends[0:1, samples - 1 : samples]
    size = jnp.exp(diff[0:1])
    sin, cos = sincos(diff[1:2])
    contrib = [jnp.where(used, weight * (size * cos), 0.0), jnp.where(used, weight * (size * sin), 0.0)]
    splits = [parts3(x) for x in contrib]
    e_rows = pack_rows([splits[i][j] for j in range(3) for i in range(2)], 16).astype(BF16)
    energy = nn(e_rows, pick[...])
    energy = energy[0:2] + energy[2:4] + energy[4:6]
    e_msg[...] = jnp.zeros_like(e_msg)
    e_msg[0:2, :samples] = energy

    def e_copy(d):
        return pltpu.make_async_remote_copy(
            src_ref=e_msg,
            dst_ref=e_buf.at[l],
            send_sem=e_send.at[d],
            recv_sem=e_recv.at[l],
            device_id=member(k, lax.rem(l + d, cn)),
            device_id_type=MESH,
        )

    def send_e(d, carry):
        e_copy(d).start()
        return carry

    lax.fori_loop(1, cn, send_e, 0)
    e_buf[l] = e_msg[...]

    for d in range(1, g):
        pltpu.make_async_remote_copy(
            src_ref=occ_mine,
            dst_ref=occ_col.at[lax.rem(q + d, g)],
            send_sem=col_send.at[d],
            recv_sem=col_recv.at[d],
            device_id=(b, p_core),
            device_id_type=MESH,
        ).wait_recv()
    for i in range(g):

        @pl.when(jnp.logical_not(alone & (q == i)))
        def _():
            pltpu.make_async_remote_copy(
                src_ref=occ_mine,
                dst_ref=occ_row.at[i],
                send_sem=row_send.at[0],
                recv_sem=row_recv.at[i],
                device_id=(b, p_core),
                device_id_type=MESH,
            ).wait_recv()

    def hidden_of(ref):
        rows = ref[...].reshape(block, ref.shape[2])[:, :orbitals]
        return jnp.tanh(nn(rows, w1) + bias).astype(BF16)

    def slope_of(hid):
        mid = jnp.tanh(nn(hid, w2))
        return 1.0 - mid * mid

    hid_k = hidden_of(occ_col)
    hid_l = hidden_of(occ_row)
    slope_k = slope_of(hid_k)
    slope_l = slope_of(hid_l)
    gram = nt(hid_k, hid_l)
    l_hi = slope_l.astype(BF16)
    l_lo = (slope_l - l_hi.astype(F32)).astype(BF16)
    ones = []
    pairs = (readout[0:1] * readout[0:1], readout[0:1] * readout[1:2], readout[1:2] * readout[1:2])
    for t, pair in enumerate(pairs):
        scaled = slope_k * pair
        s_hi = scaled.astype(BF16)
        s_lo = (scaled - s_hi.astype(F32)).astype(BF16)
        kt = gram * (nt(s_hi, l_hi) + (nt(s_lo, l_hi) + nt(s_hi, l_lo)))
        hi = kt.astype(BF16)
        kt_hi[t] = hi
        kt_lo[t] = (kt - hi.astype(F32)).astype(BF16)
        ones.append(jnp.sum(kt, axis=0, keepdims=True))

    def apply(va, vb):
        ma = jnp.sum(va, axis=1, keepdims=True) * (1.0 / block)
        mb = jnp.sum(vb, axis=1, keepdims=True) * (1.0 / block)
        rows = pack_rows([*parts3(va - ma), *parts3(vb - mb)], 16).astype(BF16)
        outs = []
        for t in range(3):
            out = nn(rows, kt_hi[t]) + nn(rows, kt_lo[t])
            outs.append((out[0:1] + out[1:2] + out[2:3], out[3:4] + out[4:5] + out[5:6]))
        y_re = outs[0][0] + outs[1][1] + (ones[0] * ma + ones[1] * mb)
        y_im = outs[1][0] + outs[2][1] + (ones[1] * ma + ones[2] * mb)
        return y_re, y_im

    def across(msg, buf, send, recv):
        def copy(d):
            return pltpu.make_async_remote_copy(
                src_ref=msg,
                dst_ref=buf.at[k],
                send_sem=send.at[d],
                recv_sem=recv.at[k],
                device_id=member(l, lax.rem(l + d, cn)),
                device_id_type=MESH,
            )

        def begin(d, carry):
            copy(d).start()
            return carry

        lax.fori_loop(1, cn, begin, 0)

        @pl.when(jnp.logical_not(alone))
        def _():
            copy(0).start()

        @pl.when(alone)
        def _():
            buf[k] = msg[...]

        def arrived(j):
            pltpu.make_async_remote_copy(
                src_ref=msg,
                dst_ref=buf.at[j],
                send_sem=send.at[0],
                recv_sem=recv.at[j],
                device_id=(b, p_core),
                device_id_type=MESH,
            ).wait_recv()

        def finish(d, carry):
            arrived(lax.rem(k + d, cn))
            return carry

        lax.fori_loop(1, cn, finish, 0)

        @pl.when(jnp.logical_not(alone))
        def _():
            arrived(k)

    def drain(msg, buf, send):
        def one(d):
            pltpu.make_async_remote_copy(
                src_ref=msg,
                dst_ref=buf.at[k],
                send_sem=send.at[d],
                recv_sem=send.at[d],
                device_id=(b, p_core),
                device_id_type=MESH,
            ).wait_send()

        def step(d, carry):
            one(d)
            return carry

        lax.fori_loop(1, cn, step, 0)

        @pl.when(jnp.logical_not(alone))
        def _():
            one(0)

    def e_wait(d, carry):
        pltpu.make_async_remote_copy(
            src_ref=e_msg,
            dst_ref=e_buf.at[lax.rem(l + d, cn)],
            send_sem=e_send.at[0],
            recv_sem=e_recv.at[lax.rem(l + d, cn)],
            device_id=(b, p_core),
            device_id_type=MESH,
        ).wait_recv()
        return carry

    lax.fori_loop(1, cn, e_wait, 0)
    sums = []
    for i in range(g):
        acc = e_buf[i * pn]
        for j in range(1, pn):
            acc = acc + e_buf[i * pn + j]
        sums.append(acc)
    tiles = [sums[i] + pltpu.roll(sums[i + 1], samples, 1) for i in range(0, g, 2)]
    energies = jnp.concatenate(tiles, axis=1)
    mine = e_buf[q * pn]
    for j in range(1, pn):
        mine = mine + e_buf[q * pn + j]
    out_ref[0:2] = mine[0:2]

    ea = energies[1:2] * (1.0 / total)
    eb = energies[0:1] * (-1.0 / total)
    y_re, y_im = apply(ea, eb)
    ma = jnp.broadcast_to(jnp.sum(ea, axis=1, keepdims=True) * (1.0 / total), ea.shape)
    mb = jnp.broadcast_to(jnp.sum(eb, axis=1, keepdims=True) * (1.0 / total), eb.shape)
    y_msg[...] = pack_rows([y_re, y_im, *ones, ma, mb], 8)
    across(y_msg, y_buf, y_send, y_recv)
    y = y_buf[0]
    for j in range(1, cn):
        y = y + y_buf[j]
    one_rr, one_ri, one_ii = y[2:3], y[3:4], y[4:5]
    ga, gb = y[5:6], y[6:7]
    fa, fb = ea - ga, eb - gb
    f_re = y[0:1] - (one_rr * ga + one_ri * gb)
    f_im = y[1:2] - (one_ri * ga + one_ii * gb)

    ha = f_re * (1.0 / total) + DIAG_SHIFT * fa
    hb = f_im * (1.0 / total) + DIAG_SHIFT * fb
    z_re, z_im = apply(ha, hb)
    ma = jnp.broadcast_to(jnp.sum(f_re, axis=1, keepdims=True) * (1.0 / total), ea.shape)
    mb = jnp.broadcast_to(jnp.sum(f_im, axis=1, keepdims=True) * (1.0 / total), eb.shape)
    z_msg[...] = pack_rows([z_re, z_im, ma, mb], 8)
    across(z_msg, z_buf, z_send, z_recv)
    z = z_buf[0]
    for j in range(1, cn):
        z = z + z_buf[j]
    f_mean_re, f_mean_im = z[2:3], z[3:4]
    ga, gb = f_mean_re * (1.0 / total), f_mean_im * (1.0 / total)
    a_re = z[0:1] - (one_rr * ga + one_ri * gb)
    a_im = z[1:2] - (one_ri * ga + one_ii * gb)
    ha, hb = ha - ga, hb - gb

    def inner(ua, ub, va, vb):
        return jnp.sum(ua * va + ub * vb, axis=1, keepdims=True)

    mean_re = jnp.sum(a_re, axis=1, keepdims=True) * (1.0 / block)
    mean_im = jnp.sum(a_im, axis=1, keepdims=True) * (1.0 / block)
    da, db = a_re - mean_re, a_im - mean_im
    scalars = [
        inner(fa, fb, f_re, f_im),
        inner(fa, fb, a_re, a_im),
        inner(ha, hb, a_re, a_im),
        inner(da, db, da, db),
        mean_re,
        mean_im,
    ]
    s_msg[...] = pack_rows([jnp.broadcast_to(x, (1, 128)) for x in scalars], 8)
    across(s_msg, s_buf, s_send, s_recv)
    s = s_buf[0]
    for j in range(1, cn):
        s = s + s_buf[j]
    means = s * (1.0 / cn)
    spread = jnp.square(s_buf[0] - means)
    for j in range(1, cn):
        spread = spread + jnp.square(s_buf[j] - means)
    ff, f_af, af_af = s[0:1, 0:1], s[1:2, 0:1], s[2:3, 0:1]
    centered = s[3:4, 0:1] + float(block) * (spread[4:5, 0:1] + spread[5:6, 0:1])
    af_aaf = centered * (1.0 / total) + DIAG_SHIFT * af_af
    alpha0 = ff / f_af
    rr = ff - 2.0 * alpha0 * f_af + alpha0 * alpha0 * af_af
    beta = rr / ff
    near = 1.0 + beta
    curv = near * near * f_af - 2.0 * near * alpha0 * af_af + alpha0 * alpha0 * af_aaf
    alpha1 = rr / curv
    on_f = alpha0 + alpha1 * near
    on_af = alpha1 * alpha0
    pf_re, pf_im = f_re - f_mean_re, f_im - f_mean_im
    pa_re, pa_im = a_re - means[4:5, 0:1], a_im - means[5:6, 0:1]
    change = pack_rows([on_f * pf_re - on_af * pa_re, on_f * pf_im - on_af * pa_im], 8)
    for i in range(block // 128):
        change_buf[i] = change[:, i * 128 : (i + 1) * 128]
    tile = change_buf[(q * samples) // 128]
    odd = jnp.full(tile.shape, q % 2, jnp.int32) == 1
    tile = jnp.where(odd, pltpu.roll(tile, samples, 1), tile)
    out_ref[2:4] = tile[0:2]

    for copy in copies:
        copy.wait_send()
    for t in range(cn // pn):

        @pl.when(jnp.logical_not(alone & (k == p + pn * t)))
        def _():
            row_copy(t).wait_send()

    def e_drain(d, carry):
        e_copy(d).wait_send()
        return carry

    lax.fori_loop(1, cn, e_drain, 0)
    drain(y_msg, y_buf, y_send)
    drain(z_msg, z_buf, z_send)
    drain(s_msg, s_buf, s_send)


def body(n_params, n_samples, occ, counts, orb, elem, step, w1, bias, w2, readout):
    devices = n_params * n_samples
    cn = 1
    while cn * cn < devices:
        cn *= 2
    g = cn // n_params
    samples = occ.shape[0]
    slots = orb.shape[1]
    depth, hid2 = w2.shape
    hid = w1.shape[1]
    block = g * samples
    vmem = pl.BlockSpec(memory_space=pltpu.VMEM)
    dma = pltpu.SemaphoreType.DMA
    out = pl.pallas_call(
        functools.partial(kernel, n_params, cn),
        out_shape=jax.ShapeDtypeStruct((4, 128), F32),
        in_specs=[vmem, vmem, vmem, vmem, pl.BlockSpec(memory_space=pltpu.SMEM), vmem, vmem, vmem, vmem],
        out_specs=vmem,
        scratch_shapes=[
            pltpu.VMEM((samples, 256), BF16),
            pltpu.VMEM((g, samples, 256), BF16),
            pltpu.VMEM((g, samples, 256), BF16),
            pltpu.VMEM((depth * n_params, hid2), BF16),
            pltpu.VMEM((slots, hid), BF16),
            pltpu.VMEM((slots, samples), BF16),
            pltpu.VMEM((3, block, block), BF16),
            pltpu.VMEM((3, block, block), BF16),
            pltpu.VMEM((8, 128), F32),
            pltpu.VMEM((cn, 8, 128), F32),
            pltpu.VMEM((8, block), F32),
            pltpu.VMEM((cn, 8, block), F32),
            pltpu.VMEM((8, block), F32),
            pltpu.VMEM((cn, 8, block), F32),
            pltpu.VMEM((8, 128), F32),
            pltpu.VMEM((cn, 8, 128), F32),
            pltpu.VMEM((block // 128, 8, 128), F32),
            dma((5,)),
            dma((5,)),
            dma((g,)),
            dma((g,)),
            dma((cn // n_params,)),
            dma((g,)),
            dma((cn,)),
            dma((cn,)),
            dma((cn,)),
            dma((cn,)),
            dma((cn,)),
            dma((cn,)),
            dma((cn,)),
            dma((cn,)),
        ],
        compiler_params=pltpu.CompilerParams(
            collective_id=0, has_side_effects=True, vmem_limit_bytes=40 * 1024 * 1024
        ),
    )(
        occ,
        counts.reshape(1, samples),
        orb,
        elem,
        step.reshape(1, 1),
        w1,
        bias.reshape(1, hid),
        w2,
        readout,
    )
    return out[0:2, :samples], out[2:4, :samples]


def solution(mesh):
    return jax.shard_map(
        functools.partial(body, mesh.shape["params"], mesh.shape["samples"]),
        mesh=mesh,
        in_specs=(
            P("samples", None),
            P("samples"),
            P(None, ("samples", "params")),
            P(None, ("samples", "params")),
            P(),
            P(),
            P(),
            P("params", None),
            P(),
        ),
        out_specs=(P(None, "samples"), P(None, "samples")),
        check_vma=False,
    )
```

time: 2270 us -> 69.6 us (0.03)
  waiting for transfers between devices: 1880 us -> 0 us
  blocking collectives: 301 us -> 0 us
  Pallas kernels: 0 us -> 62 us
  local copies, waits for them, and re-layouts: 35.8 us -> 6 us
    psum x3 -> x0, waiting for transfers between devices: 1880 us -> none  [the longest x2 1220 us: body(): lax.psum(jnp.dot(hidden_part.T, back, precision=PRECISE), 'samples')]
    psum x8 -> x0, blocking collectives: 291 us -> none  [the longest x1 156 us: body(): energy_sum = lax.psum(jnp.sum(local_energy, axis=1), 'samples')]
    pallas_call x0 -> x1, Pallas kernels: none -> 62 us  [body(): pl.pallas_call(functools.partial(kernel, n_params, cn), out_shape=jax.Sha...]
    gather x18 -> x0, local copies, waits for them, and re-layouts: 33.8 us -> none  [the longest x5 25.6 us: body(): jnp.take_along_axis(jnp.take(occupations, parents, axis=0), connection_or...]
  transfers between devices with their start and end apart: 3 -> 0, of which waited for: 3 -> 0; matrix products, arithmetic and copies ran while one was open for 0% -> 0% of each run, Pallas kernels for 0% -> 0%
where the time goes in v1:
time: 69.6 us; the launch traced here: 69.3 us
  Pallas kernels  62 us (89%)
  local copies, waits for them, and re-layouts  6 us (9%)
  between operations  1.32 us (2%)
    pallas_call x1, Pallas kernels, body(): pl.pallas_call(functools.partial(kernel, n_params, cn), out_shape=jax.Sha...  62 us
    unnamed x16, local copies, waits for them, and re-layouts  5.43 us

profile of v1, /device:TPU:1, one launch (start us, length us, event | category | flops | bytes accessed | tf_op | source)
XLA Modules:
  0.0 69.3 jit_solution(8295124735479887498)
XLA Ops:
  0.6 0.0 copy-start.4
  1.3 0.0 copy-start.7
  1.3 0.0 copy-done.4
  1.3 0.6 copy-done.7
  2.0 0.0 copy-start
  2.0 1.0 %copy-done = bf16[152,1024]{1,0:T(8,128)(2,1)S(1)} copy-done((bf16[152,1024]{1,0:T(8,128)(2,1)S(1)}, bf16[152,1024]{1,0:T(8,128)(2,1)}, u32[]{:S(2)}) %copy-start) | copy-done | bytes 311320
  2.9 0.0 copy-start.1
  2.9 0.9 %copy-done.1 = bf16[256,256]{1,0:T(8,128)(2,1)S(1)} copy-done((bf16[256,256]{1,0:T(8,128)(2,1)S(1)}, bf16[256,256]{1,0:T(8,128)(2,1)}, u32[]{:S(2)}) %copy-start.1) | copy-done | bytes 131096
  3.8 0.0 copy-start.2
  3.8 0.8 %copy-done.2 = s32[64,152]{1,0:T(8,128)S(1)} copy-done((s32[64,152]{1,0:T(8,128)S(1)}, s32[64,152]{1,0:T(8,128)}, u32[]{:S(2)}) %copy-start.2) | copy-done | bytes 38936
  4.7 0.0 copy-start.3
  4.7 0.7 %copy-done.3 = s32[4,768]{1,0:T(4,128)S(1)} copy-done((s32[4,768]{1,0:T(4,128)S(1)}, s32[4,768]{1,0:T(4,128)}, u32[]{:S(2)}) %copy-start.3) | copy-done | bytes 12312
  5.4 0.0 copy-start.5
  5.4 0.7 copy-done.5
  6.1 0.0 copy-start.6
  6.1 0.7 copy-done.6
  6.7 62.0 %shard_map.104 = f32[4,128]{1,0:T(4,128)S(1)} custom-call(s32[64,152]{1,0:T(8,128)S(1)} %copy-done.2, s32[1,64]{1,0:T(1,128)S(1)} %bitcast.5, s32[4,768]{1,0:T(4,128)S(1)} %copy-done.3, f32[2,768]{1,0:T(2,128)S(1)} %copy-done.4, s32[1,1]{1,0:T(1,128)} %bitcast.3.step_ref, bf16[152,1024]{1,0:T(8,128)(2,1)S(1)} %copy-done, f32[1,1024]{1,0:T(1,128)S(1)} %bitcast.4, ...), custom_call_target="tpu_custom_call" | custom-call | tf_op jit(solution)/shard_map/pallas_call | solution.py:549
  68.7 0.6 fusion
Async XLA Ops:
  0.6 0.7 copy-start.4
  1.3 0.7 copy-start.7
  2.0 1.0 %copy-start = (bf16[152,1024]{1,0:T(8,128)(2,1)S(1)}, bf16[152,1024]{1,0:T(8,128)(2,1)}, u32[]{:S(2)}) copy-start(bf16[152,1024]{1,0:T(8,128)(2,1)} %w1_ref.1) | copy-start | bytes 933892
  2.9 0.9 %copy-start.1 = (bf16[256,256]{1,0:T(8,128)(2,1)S(1)}, bf16[256,256]{1,0:T(8,128)(2,1)}, u32[]{:S(2)}) copy-start(bf16[256,256]{1,0:T(8,128)(2,1)} %w2_ref.1) | copy-start | bytes 393220
  3.8 0.8 %copy-start.2 = (s32[64,152]{1,0:T(8,128)S(1)}, s32[64,152]{1,0:T(8,128)}, u32[]{:S(2)}) copy-start(s32[64,152]{1,0:T(8,128)} %occ_ref.1) | copy-start | bytes 116740
  4.7 0.7 %copy-start.3 = (s32[4,768]{1,0:T(4,128)S(1)}, s32[4,768]{1,0:T(4,128)}, u32[]{:S(2)}) copy-start(s32[4,768]{1,0:T(4,128)} %orb_ref.1) | copy-start | bytes 36868
  5.4 0.7 copy-start.5
  6.1 0.7 copy-start.6

commit v2 on v1

v2 whole, which is shorter than its diff:
```python
import jax
import jax.numpy as jnp
from jax import lax
from jax.experimental import pallas as pl
from jax.experimental.pallas import tpu as pltpu
from jax.sharding import PartitionSpec as P

FIELD_SCALE = 0.8
FIELD_RATE = 0.0123
DIAG_SHIFT = 0.01
LINE = 8
PLANE = 8
PARAMS = 4
MESH = pl.DeviceIdType.MESH
F32 = jnp.float32
BF16 = jnp.bfloat16


def sincos(x):
    n = jnp.floor(x * 0.6366197723675814 + 0.5)
    r = x - n * 1.5703125
    r = r - n * 4.8351287841796875e-4
    r = r - n * 3.1385570764541626e-7
    r = r - n * 6.0771005065061922e-11
    z = r * r
    s = r + r * z * (-1.6666654611e-1 + z * (8.3321608736e-3 - z * 1.9515295891e-4))
    c = 1.0 - 0.5 * z + z * z * (
        4.166664568298827e-2 + z * (-1.388731625493765e-3 + z * 2.443315711809948e-5)
    )
    quad = n - 4.0 * jnp.floor(n * 0.25)
    odd = (quad == 1.0) | (quad == 3.0)
    sin = jnp.where(odd, c, s)
    cos = jnp.where(odd, s, c)
    sin = jnp.where(quad >= 2.0, -sin, sin)
    cos = jnp.where((quad == 1.0) | (quad == 2.0), -cos, cos)
    return sin, cos


def parts3(x):
    hi = x.astype(BF16).astype(F32)
    rest = x - hi
    mid = rest.astype(BF16).astype(F32)
    return hi, mid, rest - mid


def pack_rows(rows, height):
    width = rows[0].shape[1]
    place = lax.broadcasted_iota(jnp.int32, (height, width), 0)
    out = jnp.zeros((height, width), F32)
    for i, row in enumerate(rows):
        out = jnp.where(place == i, jnp.broadcast_to(row, (height, width)), out)
    return out


def nn(a, b):
    return lax.dot_general(a, b, (((1,), (0,)), ((), ())), preferred_element_type=F32)


def nt(a, b):
    return lax.dot_general(a, b, (((1,), (1,)), ((), ())), preferred_element_type=F32)


def tn(a, b):
    return lax.dot_general(a, b, (((0,), (0,)), ((), ())), preferred_element_type=F32)


def kernel(
    occ_hbm,
    counts_hbm,
    orb_hbm,
    elem_hbm,
    step_hbm,
    w1_hbm,
    bias_hbm,
    w2_hbm,
    readout_hbm,
    out_ref,
    occ_ref,
    counts_ref,
    orb_ref,
    elem_ref,
    step_ref,
    w1_ref,
    bias_ref,
    w2_ref,
    readout_ref,
    in_sem,
    occ_mine,
    occ_line,
    occ_plane,
    w2_full,
    slot_hid,
    pick,
    kt_hi,
    kt_lo,
    e_msg,
    e_buf,
    kp_msg,
    kp_buf,
    kl_msg,
    kl_buf,
    y_msg,
    y_buf,
    z_msg,
    z_buf,
    s_msg,
    s_buf,
    own_buf,
    w2_send,
    w2_recv,
    op_send,
    op_recv,
    ol_send,
    ol_recv,
    e_send,
    e_recv,
    kp_send,
    kp_recv,
    kl_send,
    kl_recv,
    y_send,
    y_recv,
    z_send,
    z_recv,
    s_send,
    s_recv,
):
    outside = (occ_hbm, w2_hbm, w1_hbm, orb_hbm, counts_hbm, bias_hbm, elem_hbm, step_hbm, readout_hbm)
    inside = (occ_ref, w2_ref, w1_ref, orb_ref, counts_ref, bias_ref, elem_ref, step_ref, readout_ref)
    loads = [pltpu.make_async_copy(a, c, in_sem.at[i]) for i, (a, c) in enumerate(zip(outside, inside))]
    for load in loads:
        load.start()
    samples, orbitals = occ_ref.shape
    slots = orb_ref.shape[1]
    depth = w2_ref.shape[0]
    pn = PARAMS
    block = LINE * samples
    total = float(block * PLANE)

    b = lax.axis_index("samples")
    p = lax.axis_index("params")
    z = b // PLANE
    w = b % PLANE
    p_core = p + 1 - 2 * (p % 2)
    p_far = p + 2 - 4 * (p // 2)
    p_cross = p_far + 1 - 2 * (p_far % 2)
    b_pair = b + 1 - 2 * (b % 2)

    def line_peer(d):
        to = lax.rem(z + d, LINE)
        return to, (to * PLANE + w, p)

    def plane_peer(d):
        y, half = w // 2, w % 2
        to_y = lax.rem(y + d // 2, PLANE // 2)
        if d % 2:
            to = to_y * 2 + 1 - half
            return to, (z * PLANE + to, p_far)
        to = to_y * 2 + half
        return to, (z * PLANE + to, p)

    LINE_ORDER = (4, 3, 5, 2, 6, 1, 7)
    PLANE_ORDER = (5, 4, 3, 7, 2, 6, 1)

    def energy_peer(d):
        return lax.rem(z + d // pn, LINE) * PLANE + w, lax.rem(p + lax.rem(d, pn), pn)

    def copy_to(src, dst, send, recv, device):
        return pltpu.make_async_remote_copy(
            src_ref=src, dst_ref=dst, send_sem=send, recv_sem=recv, device_id=device, device_id_type=MESH
        )

    def spread(peer, order, me, msg, buf, send, recv):
        for d in order:
            copy_to(msg, buf.at[me], send.at[d], recv.at[me], peer(d)[1]).start()
        buf[me] = msg[...]

    def collect(peer, order, msg, buf, send, recv):
        for d in order:
            place, device = peer(d)
            copy_to(msg, buf.at[place], send.at[d], recv.at[place], device).wait_recv()

    def drain(peer, order, me, msg, buf, send, recv):
        for d in order:
            copy_to(msg, buf.at[me], send.at[d], recv.at[me], peer(d)[1]).wait_send()

    line = (line_peer, LINE_ORDER)
    plane = (plane_peer, PLANE_ORDER)

    barrier = pltpu.get_barrier_semaphore()

    def signal(device):
        pl.semaphore_signal(barrier, inc=1, device_id=device, device_id_type=MESH)

    signal((b_pair, p_cross))
    for d in PLANE_ORDER:
        signal(plane_peer(d)[1])

    def greet(d, carry):
        signal(energy_peer(d))
        return carry

    lax.fori_loop(1, LINE * pn, greet, 0)

    loads[0].wait()
    occ = occ_ref[...].astype(F32)
    occ_mine[...] = jnp.zeros_like(occ_mine)
    occ_mine[:, :orbitals] = occ.astype(BF16)
    loads[1].wait()

    pl.semaphore_wait(barrier, LINE * pn - 1 + PLANE - 1 + 1)

    half = depth // 2
    whole = pl.ds(pl.multiple_of(p * depth, depth), depth)
    w2_copies = []
    for d, far in ((0, p_far), (1, p_cross)):
        for h, to in ((0, b), (1, b_pair)):
            rows = pl.ds(pl.multiple_of(p * depth + h * half, half), half)
            i = 1 + d * 2 + h
            w2_copies.append(
                copy_to(w2_ref.at[pl.ds(h * half, half)], w2_full.at[rows], w2_send.at[i], w2_recv.at[i], (to, far))
            )
    w2_copies.append(copy_to(w2_ref, w2_full.at[whole], w2_send.at[0], w2_recv.at[0], (b, p_core)))
    for copy in w2_copies:
        copy.start()
    spread(*plane, w, occ_mine, occ_plane, op_send, op_recv)
    spread(*line, z, occ_mine, occ_line, ol_send, ol_recv)
    w2_full[whole] = w2_ref[...]

    for load in loads[2:]:
        load.wait()
    counts = jnp.broadcast_to(counts_ref[...].astype(F32), (8, samples))
    r_id = lax.broadcasted_iota(jnp.int32, (samples, samples), 0)
    c_id = lax.broadcasted_iota(jnp.int32, (samples, samples), 1)
    upto = (r_id <= c_id).astype(BF16)
    c_hi, c_mid, c_lo = parts3(counts)
    ends = nn(c_hi.astype(BF16), upto) + nn(c_mid.astype(BF16), upto) + nn(c_lo.astype(BF16), upto)
    begins = ends - counts
    ends, begins = ends[0:1], begins[0:1]
    position = (p + pn * lax.broadcasted_iota(jnp.int32, (slots, samples), 0)).astype(F32)
    pick[...] = ((begins <= position) & (position < ends)).astype(BF16)
    occ_t = occ.T.astype(BF16)
    w1 = w1_ref[...]
    bias = bias_ref[...]
    chunk = 256
    for start_row in range(0, slots, chunk):
        rows = slice(start_row, start_row + chunk)
        base = nt(occ_t, pick[rows])
        column = lax.broadcasted_iota(jnp.int32, (orbitals, chunk), 0)
        orb = orb_ref[:, rows]
        flip = orb[0:1] == column
        for u in range(1, orb_ref.shape[0]):
            flip = flip | (orb[u : u + 1] == column)
        flipped = jnp.where(flip, 1.0 - base, base).astype(BF16)
        slot_hid[rows] = jnp.tanh(tn(flipped, w1) + bias).astype(BF16)
    hidden = jnp.tanh(nn(occ_mine[:, :orbitals], w1) + bias).astype(BF16)

    for copy in w2_copies:
        copy.wait_recv()
    w2 = w2_full[...]

    readout = readout_ref[...]
    r_rows = pack_rows([x[i : i + 1] for x in parts3(readout) for i in range(2)], 16).astype(BF16)

    def logs_of(hid):
        mid = jnp.tanh(nn(hid, w2))
        hi = mid.astype(BF16)
        lo = (mid - hi.astype(F32)).astype(BF16)
        out = nt(r_rows, hi) + nt(r_rows, lo)
        return out[0:2] + out[2:4] + out[4:6]

    logs = logs_of(hidden)
    slot_logs = logs_of(slot_hid[...])
    l_rows = pack_rows([x[i : i + 1] for x in parts3(logs) for i in range(2)], 16).astype(BF16)
    parent_logs = nt(l_rows, pick[...])
    parent_logs = parent_logs[0:2] + parent_logs[2:4] + parent_logs[4:6]
    diff = slot_logs - parent_logs
    angle = jnp.broadcast_to(step_ref[...].astype(F32), (1, slots)) * FIELD_RATE
    field = FIELD_SCALE * sincos(angle)[0]
    elem = elem_ref[...]
    weight = elem[0:1] + field * elem[1:2]
    slot_at = (p + pn * lax.broadcasted_iota(jnp.int32, (1, slots), 1)).astype(F32)
    used = slot_at < ends[0:1, samples - 1 : samples]
    size = jnp.exp(diff[0:1])
    sin, cos = sincos(diff[1:2])
    contrib = [jnp.where(used, weight * (size * cos), 0.0), jnp.where(used, weight * (size * sin), 0.0)]
    splits = [parts3(x) for x in contrib]
    e_rows = pack_rows([splits[i][j] for j in range(3) for i in range(2)], 16).astype(BF16)
    energy = nn(e_rows, pick[...])
    energy = energy[0:2] + energy[2:4] + energy[4:6]
    e_msg[...] = jnp.zeros_like(e_msg)
    e_msg[0:2, :samples] = energy

    me = z * pn + p

    def e_copy(d):
        return copy_to(e_msg, e_buf.at[me], e_send.at[d], e_recv.at[me], energy_peer(d))

    def send_e(d, carry):
        e_copy(d).start()
        return carry

    lax.fori_loop(1, LINE * pn, send_e, 0)
    e_buf[me] = e_msg[...]

    collect(*plane, occ_mine, occ_plane, op_send, op_recv)
    collect(*line, occ_mine, occ_line, ol_send, ol_recv)

    def hidden_of(ref):
        rows = ref[...].reshape(block, ref.shape[2])[:, :orbitals]
        return jnp.tanh(nn(rows, w1) + bias).astype(BF16)

    def slope_of(hid):
        mid = jnp.tanh(nn(hid, w2))
        return 1.0 - mid * mid

    hid_c = hidden_of(occ_line)
    hid_r = hidden_of(occ_plane)
    slope_c = slope_of(hid_c)
    slope_r = slope_of(hid_r)
    gram = nt(hid_c, hid_r)
    r_hi = slope_r.astype(BF16)
    r_lo = (slope_r - r_hi.astype(F32)).astype(BF16)
    ones = jnp.ones((16, block), BF16)
    ones_r, ones_c = [], []
    pairs = (readout[0:1] * readout[0:1], readout[0:1] * readout[1:2], readout[1:2] * readout[1:2])
    for t, pair in enumerate(pairs):
        scaled = slope_c * pair
        s_hi = scaled.astype(BF16)
        s_lo = (scaled - s_hi.astype(F32)).astype(BF16)
        kt = gram * (nt(s_hi, r_hi) + (nt(s_lo, r_hi) + nt(s_hi, r_lo)))
        hi = kt.astype(BF16)
        lo = (kt - hi.astype(F32)).astype(BF16)
        kt_hi[t] = hi
        kt_lo[t] = lo
        ones_r.append(jnp.sum(kt, axis=0, keepdims=True))
        ones_c.append((nt(ones, hi) + nt(ones, lo))[0:1])
    kp_msg[...] = pack_rows(ones_r, 8)
    kl_msg[...] = pack_rows(ones_c, 8)
    spread(*plane, w, kp_msg, kp_buf, kp_send, kp_recv)
    spread(*line, z, kl_msg, kl_buf, kl_send, kl_recv)

    def apply(va, vb, ones, mul):
        ma = jnp.sum(va, axis=1, keepdims=True) * (1.0 / block)
        mb = jnp.sum(vb, axis=1, keepdims=True) * (1.0 / block)
        rows = pack_rows([*parts3(va - ma), *parts3(vb - mb)], 16).astype(BF16)
        outs = []
        for t in range(3):
            out = mul(rows, kt_hi[t]) + mul(rows, kt_lo[t])
            outs.append((out[0:1] + out[1:2] + out[2:3], out[3:4] + out[4:5] + out[5:6]))
        y_re = outs[0][0] + outs[1][1] + (ones[0] * ma + ones[1] * mb)
        y_im = outs[1][0] + outs[2][1] + (ones[1] * ma + ones[2] * mb)
        return y_re, y_im

    def total_of(buf):
        acc = buf[0]
        for j in range(1, buf.shape[0]):
            acc = acc + buf[j]
        return acc

    def pieces(tiles):
        pairs = [tiles[i] + pltpu.roll(tiles[i + 1], samples, 1) for i in range(0, len(tiles), 2)]
        return jnp.concatenate(pairs, axis=1)

    lane = lax.broadcasted_iota(jnp.int32, (8, 128), 1)

    def piece(value, place):
        for i in range(block // 128):
            own_buf[i] = value[:, i * 128 : (i + 1) * 128]
        tile = own_buf[place // 2]
        odd = jnp.full(tile.shape, place % 2, jnp.int32) == 1
        tile = jnp.where(odd, pltpu.roll(tile, samples, 1), tile)
        return jnp.where(lane < samples, tile, 0.0)

    def e_wait(d, carry):
        to_b, to_p = energy_peer(d)
        place = (to_b // PLANE) * pn + to_p
        copy_to(e_msg, e_buf.at[place], e_send.at[d], e_recv.at[place], (to_b, to_p)).wait_recv()
        return carry

    lax.fori_loop(1, LINE * pn, e_wait, 0)

    def over_params(i):
        acc = e_buf[i * pn]
        for j in range(1, pn):
            acc = acc + e_buf[i * pn + j]
        return acc

    energies = pieces([over_params(i) for i in range(LINE)])
    mine = over_params(z)
    out_ref[0:2] = mine[0:2]

    ea = energies[1:2] * (1.0 / total)
    eb = energies[0:1] * (-1.0 / total)
    y_re, y_im = apply(ea, eb, ones_r, nn)
    y_msg[0:8] = pack_rows([y_re, y_im], 8)
    y_msg[2:4, 0:128] = mine[0:2]
    means = [jnp.sum(v, axis=1, keepdims=True) * (1.0 / total) for v in (ea, eb)]
    y_msg[2:4, 128:256] = pack_rows([jnp.broadcast_to(v, (1, 128)) for v in means], 2)
    spread(*plane, w, y_msg, y_buf, y_send, y_recv)
    collect(*plane, kp_msg, kp_buf, kp_send, kp_recv)
    collect(*plane, y_msg, y_buf, y_send, y_recv)
    k1 = total_of(kp_buf)
    y = total_of(y_buf)
    ga, gb = y[2:3, 128:129], y[3:4, 128:129]
    around = pieces([y_buf[i, :, 0:128] for i in range(PLANE)])
    fa = around[3:4] * (1.0 / total) - ga
    fb = around[2:3] * (-1.0 / total) - gb
    f_re = y[0:1] - (k1[0:1] * ga + k1[1:2] * gb)
    f_im = y[1:2] - (k1[1:2] * ga + k1[2:3] * gb)

    ha = f_re * (1.0 / total) + DIAG_SHIFT * fa
    hb = f_im * (1.0 / total) + DIAG_SHIFT * fb
    z_re, z_im = apply(ha, hb, ones_c, nt)
    z_msg[0:8] = pack_rows([z_re, z_im], 8)
    f_mine = piece(pack_rows([f_re, f_im], 8), w)
    z_msg[2:4, 0:128] = f_mine[0:2]
    norm = jnp.sum(fa * f_re + fb * f_im, axis=1, keepdims=True)
    means = [jnp.sum(v, axis=1, keepdims=True) * (1.0 / total) for v in (f_re, f_im)]
    z_msg[2:5, 128:256] = pack_rows([jnp.broadcast_to(v, (1, 128)) for v in (*means, norm)], 3)
    spread(*line, z, z_msg, z_buf, z_send, z_recv)
    ca, cb = ea - ga, eb - gb
    collect(*line, kl_msg, kl_buf, kl_send, kl_recv)
    collect(*line, z_msg, z_buf, z_send, z_recv)
    k1 = total_of(kl_buf)
    acc = total_of(z_buf)
    f_mean_re, f_mean_im, ff = acc[2:3, 128:129], acc[3:4, 128:129], acc[4:5, 128:129]
    ga, gb = f_mean_re * (1.0 / total), f_mean_im * (1.0 / total)
    a_re = acc[0:1] - (k1[0:1] * ga + k1[1:2] * gb)
    a_im = acc[1:2] - (k1[1:2] * ga + k1[2:3] * gb)
    along = pieces([z_buf[i, :, 0:128] for i in range(LINE)])
    ha = along[2:3] * (1.0 / total) - ga + DIAG_SHIFT * ca
    hb = along[3:4] * (1.0 / total) - gb + DIAG_SHIFT * cb

    def inner(ua, ub, va, vb):
        return jnp.sum(ua * va + ub * vb, axis=1, keepdims=True)

    mean_re = jnp.sum(a_re, axis=1, keepdims=True) * (1.0 / block)
    mean_im = jnp.sum(a_im, axis=1, keepdims=True) * (1.0 / block)
    da, db = a_re - mean_re, a_im - mean_im
    scalars = [
        inner(ca, cb, a_re, a_im),
        inner(ha, hb, a_re, a_im),
        inner(da, db, da, db),
        mean_re,
        mean_im,
    ]
    s_msg[...] = pack_rows([jnp.broadcast_to(x, (1, 128)) for x in scalars], 8)
    spread(*plane, w, s_msg, s_buf, s_send, s_recv)
    a_mine = piece(pack_rows([a_re, a_im], 8), z)

    for copy in w2_copies:
        copy.wait_send()

    def e_drain(d, carry):
        e_copy(d).wait_send()
        return carry

    lax.fori_loop(1, LINE * pn, e_drain, 0)
    drain(*plane, w, occ_mine, occ_plane, op_send, op_recv)
    drain(*line, z, occ_mine, occ_line, ol_send, ol_recv)
    drain(*plane, w, kp_msg, kp_buf, kp_send, kp_recv)
    drain(*line, z, kl_msg, kl_buf, kl_send, kl_recv)
    drain(*plane, w, y_msg, y_buf, y_send, y_recv)
    drain(*line, z, z_msg, z_buf, z_send, z_recv)

    collect(*plane, s_msg, s_buf, s_send, s_recv)
    s = total_of(s_buf)
    means = s * (1.0 / PLANE)
    spread_sq = jnp.square(s_buf[0] - means)
    for j in range(1, PLANE):
        spread_sq = spread_sq + jnp.square(s_buf[j] - means)
    f_af, af_af = s[0:1, 0:1], s[1:2, 0:1]
    centered = s[2:3, 0:1] + float(block) * (spread_sq[3:4, 0:1] + spread_sq[4:5, 0:1])
    af_aaf = centered * (1.0 / total) + DIAG_SHIFT * af_af
    alpha0 = ff / f_af
    rr = ff - 2.0 * alpha0 * f_af + alpha0 * alpha0 * af_af
    beta = rr / ff
    near = 1.0 + beta
    curv = near * near * f_af - 2.0 * near * alpha0 * af_af + alpha0 * alpha0 * af_aaf
    alpha1 = rr / curv
    on_f = alpha0 + alpha1 * near
    on_af = alpha1 * alpha0
    out_ref[2:3] = on_f * (f_mine[0:1] - f_mean_re) - on_af * (a_mine[0:1] - means[3:4, 0:1])
    out_ref[3:4] = on_f * (f_mine[1:2] - f_mean_im) - on_af * (a_mine[1:2] - means[4:5, 0:1])
    drain(*plane, w, s_msg, s_buf, s_send, s_recv)


def body(occ, counts, orb, elem, step, w1, bias, w2, readout):
    samples = occ.shape[0]
    slots = orb.shape[1]
    depth, hid2 = w2.shape
    hid = w1.shape[1]
    block = LINE * samples
    vmem = pl.BlockSpec(memory_space=pltpu.VMEM)
    hbm = pl.BlockSpec(memory_space=pltpu.HBM)
    dma = pltpu.SemaphoreType.DMA
    inputs = (
        occ,
        counts.reshape(1, samples),
        orb,
        elem,
        step.reshape(1, 1),
        w1,
        bias.reshape(1, hid),
        w2,
        readout,
    )

    def message(n, width):
        return [pltpu.VMEM((8, width), F32), pltpu.VMEM((n, 8, width), F32)]

    out = pl.pallas_call(
        kernel,
        out_shape=jax.ShapeDtypeStruct((4, 128), F32),
        in_specs=[hbm] * 9,
        out_specs=vmem,
        scratch_shapes=[
            *[pltpu.VMEM(x.shape, x.dtype) for x in inputs],
            dma((9,)),
            pltpu.VMEM((samples, 256), BF16),
            pltpu.VMEM((LINE, samples, 256), BF16),
            pltpu.VMEM((PLANE, samples, 256), BF16),
            pltpu.VMEM((depth * PARAMS, hid2), BF16),
            pltpu.VMEM((slots, hid), BF16),
            pltpu.VMEM((slots, samples), BF16),
            pltpu.VMEM((3, block, block), BF16),
            pltpu.VMEM((3, block, block), BF16),
            *message(LINE * PARAMS, 128),
            *message(PLANE, block),
            *message(LINE, block),
            *message(PLANE, block),
            *message(LINE, block),
            *message(PLANE, 128),
            pltpu.VMEM((block // 128, 8, 128), F32),
            dma((5,)),
            dma((5,)),
            *[dma((n,)) for n in (8, 8, 8, 8, 32, 32, 8, 8, 8, 8, 8, 8, 8, 8, 8, 8)],
        ],
        compiler_params=pltpu.CompilerParams(
            collective_id=0, has_side_effects=True, vmem_limit_bytes=61 * 1024 * 1024
        ),
    )(*inputs)
    return out[0:2, :samples], out[2:4, :samples]


def solution(mesh):
    return jax.shard_map(
        body,
        mesh=mesh,
        in_specs=(
            P("samples", None),
            P("samples"),
            P(None, ("samples", "params")),
            P(None, ("samples", "params")),
            P(),
            P(),
            P(),
            P("params", None),
            P(),
        ),
        out_specs=(P(None, "samples"), P(None, "samples")),
        check_vma=False,
    )
```

time: 69.6 us -> 45.1 us (0.65)
  Pallas kernels: 62 us -> 41.7 us
  local copies, waits for them, and re-layouts: 6 us -> 1.32 us
    pallas_call x1, Pallas kernels: 62 us -> 41.7 us  [body(): pl.pallas_call(kernel, out_shape=jax.ShapeDtypeStruct((4, 128), F32), in_...]
    unnamed x16 -> x0, local copies, waits for them, and re-layouts: 5.43 us -> none
    slice x1, local copies, waits for them, and re-layouts: 0.57 us -> 1.32 us  [body(): return (out[0:2, :samples], out[2:4, :samples])]
where the time goes in v2:
time: 45.1 us; the launch traced here: 44.3 us
  Pallas kernels  41.7 us (92%)
  local copies, waits for them, and re-layouts  1.32 us (3%)
  between operations  1.29 us (3%)
    pallas_call x1, Pallas kernels, body(): pl.pallas_call(kernel, out_shape=jax.ShapeDtypeStruct((4, 128), F32), in_...  41.7 us
    slice x1, local copies, waits for them, and re-layouts, body(): return (out[0:2, :samples], out[2:4, :samples])  1.32 us

profile of v2, /device:TPU:1, one launch (start us, length us, event | category | flops | bytes accessed | tf_op | source)
XLA Modules:
  0.0 44.3 jit_solution(3773098113799333931)
XLA Ops:
  1.3 41.7 %shard_map.104 = f32[4,128]{1,0:T(4,128)} custom-call(s32[64,152]{1,0:T(8,128)} %occ_hbm.1, s32[1,64]{1,0:T(1,128)} %bitcast.5, s32[4,768]{1,0:T(4,128)} %orb_hbm.1, f32[2,768]{1,0:T(2,128)} %elem_hbm.1, s32[1,1]{1,0:T(1,128)} %bitcast.3.step_hbm, bf16[152,1024]{1,0:T(8,128)(2,1)} %w1_hbm.1, f32[1,1024]{1,0:T(1,128)} %bitcast.4, bf16[256,256]{1,0:T(8,128)(2,1)} %w2_hbm.1, ...), custom_call_target="tpu_custom_call" | custom-call | tf_op jit(solution)/shard_map/pallas_call | solution.py:513
  43.0 1.3 %fusion = (f32[2,64]{1,0:T(2,128)}, f32[2,64]{1,0:T(2,128)}) fusion(f32[4,128]{1,0:T(4,128)} %shard_map.104), kind=kLoop, calls=%fused_computation | loop fusion | bytes 2048 | tf_op jit(solution)/shard_map/slice | solution.py:544

commit v3 on v2

--- a/solution.py
+++ b/solution.py
@@ -91,8 +91,11 @@
     w2_full,
     slot_hid,
     pick,
+    pick_t,
     kt_hi,
     kt_lo,
+    kr_hi,
+    kr_lo,
     e_msg,
     e_buf,
     kp_msg,
@@ -202,12 +205,6 @@
 
     lax.fori_loop(1, LINE * pn, greet, 0)
 
-    loads[0].wait()
-    occ = occ_ref[...].astype(F32)
-    occ_mine[...] = jnp.zeros_like(occ_mine)
-    occ_mine[:, :orbitals] = occ.astype(BF16)
-    loads[1].wait()
-
     pl.semaphore_wait(barrier, LINE * pn - 1 + PLANE - 1 + 1)
 
     half = depth // 2
@@ -218,13 +215,19 @@
             rows = pl.ds(pl.multiple_of(p * depth + h * half, half), half)
             i = 1 + d * 2 + h
             w2_copies.append(
-                copy_to(w2_ref.at[pl.ds(h * half, half)], w2_full.at[rows], w2_send.at[i], w2_recv.at[i], (to, far))
+                copy_to(w2_hbm.at[pl.ds(h * half, half)], w2_full.at[rows], w2_send.at[i], w2_recv.at[i], (to, far))
             )
-    w2_copies.append(copy_to(w2_ref, w2_full.at[whole], w2_send.at[0], w2_recv.at[0], (b, p_core)))
+    w2_copies.append(copy_to(w2_hbm, w2_full.at[whole], w2_send.at[0], w2_recv.at[0], (b, p_core)))
     for copy in w2_copies:
         copy.start()
+
+    loads[0].wait()
+    occ = occ_ref[...].astype(F32)
+    occ_mine[...] = jnp.zeros_like(occ_mine)
+    occ_mine[:, :orbitals] = occ.astype(BF16)
     spread(*plane, w, occ_mine, occ_plane, op_send, op_recv)
     spread(*line, z, occ_mine, occ_line, ol_send, ol_recv)
+    loads[1].wait()
     w2_full[whole] = w2_ref[...]
 
     for load in loads[2:]:
@@ -236,16 +239,19 @@
     c_hi, c_mid, c_lo = parts3(counts)
     ends = nn(c_hi.astype(BF16), upto) + nn(c_mid.astype(BF16), upto) + nn(c_lo.astype(BF16), upto)
     begins = ends - counts
-    ends, begins = ends[0:1], begins[0:1]
     position = (p + pn * lax.broadcasted_iota(jnp.int32, (slots, samples), 0)).astype(F32)
-    pick[...] = ((begins <= position) & (position < ends)).astype(BF16)
+    pick[...] = ((begins[0:1] <= position) & (position < ends[0:1])).astype(BF16)
+    ends_col, begins_col = ends.T[:, 0:1], begins.T[:, 0:1]
+    position = (p + pn * lax.broadcasted_iota(jnp.int32, (samples, slots), 1)).astype(F32)
+    pick_t[...] = ((begins_col <= position) & (position < ends_col)).astype(BF16)
+    ends = ends[0:1]
     occ_t = occ.T.astype(BF16)
     w1 = w1_ref[...]
     bias = bias_ref[...]
     chunk = 256
     for start_row in range(0, slots, chunk):
         rows = slice(start_row, start_row + chunk)
-        base = nt(occ_t, pick[rows])
+        base = nn(occ_t, pick_t[:, rows])
         column = lax.broadcasted_iota(jnp.int32, (orbitals, chunk), 0)
         orb = orb_ref[:, rows]
         flip = orb[0:1] == column
@@ -260,19 +266,20 @@
     w2 = w2_full[...]
 
     readout = readout_ref[...]
-    r_rows = pack_rows([x[i : i + 1] for x in parts3(readout) for i in range(2)], 16).astype(BF16)
+    r_rows = pack_rows([x[i : i + 1] for x in parts3(readout) for i in range(2)], 128)
+    r_cols = r_rows.T.astype(BF16)
 
     def logs_of(hid):
         mid = jnp.tanh(nn(hid, w2))
         hi = mid.astype(BF16)
         lo = (mid - hi.astype(F32)).astype(BF16)
-        out = nt(r_rows, hi) + nt(r_rows, lo)
+        out = (nn(hi, r_cols) + nn(lo, r_cols)).T
         return out[0:2] + out[2:4] + out[4:6]
 
     logs = logs_of(hidden)
     slot_logs = logs_of(slot_hid[...])
     l_rows = pack_rows([x[i : i + 1] for x in parts3(logs) for i in range(2)], 16).astype(BF16)
-    parent_logs = nt(l_rows, pick[...])
+    parent_logs = nn(l_rows, pick_t[...])
     parent_logs = parent_logs[0:2] + parent_logs[2:4] + parent_logs[4:6]
     diff = slot_logs - parent_logs
     angle = jnp.broadcast_to(step_ref[...].astype(F32), (1, slots)) * FIELD_RATE
@@ -296,11 +303,10 @@
     def e_copy(d):
         return copy_to(e_msg, e_buf.at[me], e_send.at[d], e_recv.at[me], energy_peer(d))
 
-    def send_e(d, carry):
-        e_copy(d).start()
-        return carry
-
-    lax.fori_loop(1, LINE * pn, send_e, 0)
+    for dz in (*LINE_ORDER, 0):
+        for dp in range(pn):
+            if dz * pn + dp:
+                e_copy(dz * pn + dp).start()
     e_buf[me] = e_msg[...]
 
     collect(*plane, occ_mine, occ_plane, op_send, op_recv)
@@ -321,7 +327,6 @@
     gram = nt(hid_c, hid_r)
     r_hi = slope_r.astype(BF16)
     r_lo = (slope_r - r_hi.astype(F32)).astype(BF16)
-    ones = jnp.ones((16, block), BF16)
     ones_r, ones_c = [], []
     pairs = (readout[0:1] * readout[0:1], readout[0:1] * readout[1:2], readout[1:2] * readout[1:2])
     for t, pair in enumerate(pairs):
@@ -334,19 +339,23 @@
         kt_hi[t] = hi
         kt_lo[t] = lo
         ones_r.append(jnp.sum(kt, axis=0, keepdims=True))
-        ones_c.append((nt(ones, hi) + nt(ones, lo))[0:1])
+        turned = kt.T
+        hi = turned.astype(BF16)
+        kr_hi[t] = hi
+        kr_lo[t] = (turned - hi.astype(F32)).astype(BF16)
+        ones_c.append(jnp.sum(turned, axis=0, keepdims=True))
     kp_msg[...] = pack_rows(ones_r, 8)
     kl_msg[...] = pack_rows(ones_c, 8)
     spread(*plane, w, kp_msg, kp_buf, kp_send, kp_recv)
     spread(*line, z, kl_msg, kl_buf, kl_send, kl_recv)
 
-    def apply(va, vb, ones, mul):
+    def apply(va, vb, ones, k_hi, k_lo):
         ma = jnp.sum(va, axis=1, keepdims=True) * (1.0 / block)
         mb = jnp.sum(vb, axis=1, keepdims=True) * (1.0 / block)
         rows = pack_rows([*parts3(va - ma), *parts3(vb - mb)], 16).astype(BF16)
         outs = []
         for t in range(3):
-            out = mul(rows, kt_hi[t]) + mul(rows, kt_lo[t])
+            out = nn(rows, k_hi[t]) + nn(rows, k_lo[t])
             outs.append((out[0:1] + out[1:2] + out[2:3], out[3:4] + out[4:5] + out[5:6]))
         y_re = outs[0][0] + outs[1][1] + (ones[0] * ma + ones[1] * mb)
         y_im = outs[1][0] + outs[2][1] + (ones[1] * ma + ones[2] * mb)
@@ -392,7 +401,7 @@
 
     ea = energies[1:2] * (1.0 / total)
     eb = energies[0:1] * (-1.0 / total)
-    y_re, y_im = apply(ea, eb, ones_r, nn)
+    y_re, y_im = apply(ea, eb, ones_r, kt_hi, kt_lo)
     y_msg[0:8] = pack_rows([y_re, y_im], 8)
     y_msg[2:4, 0:128] = mine[0:2]
     means = [jnp.sum(v, axis=1, keepdims=True) * (1.0 / total) for v in (ea, eb)]
@@ -411,7 +420,7 @@
 
     ha = f_re * (1.0 / total) + DIAG_SHIFT * fa
     hb = f_im * (1.0 / total) + DIAG_SHIFT * fb
-    z_re, z_im = apply(ha, hb, ones_c, nt)
+    z_re, z_im = apply(ha, hb, ones_c, kr_hi, kr_lo)
     z_msg[0:8] = pack_rows([z_re, z_im], 8)
     f_mine = piece(pack_rows([f_re, f_im], 8), w)
     z_msg[2:4, 0:128] = f_mine[0:2]
@@ -524,8 +533,8 @@
             pltpu.VMEM((depth * PARAMS, hid2), BF16),
             pltpu.VMEM((slots, hid), BF16),
             pltpu.VMEM((slots, samples), BF16),
-            pltpu.VMEM((3, block, block), BF16),
-            pltpu.VMEM((3, block, block), BF16),
+            pltpu.VMEM((samples, slots), BF16),
+            *[pltpu.VMEM((3, block, block), BF16)] * 4,
             *message(LINE * PARAMS, 128),
             *message(PLANE, block),
             *message(LINE, block),

time: 45.1 us -> 43.1 us (0.956)
  Pallas kernels: 41.7 us -> 39.9 us
    pallas_call x1, Pallas kernels: 41.7 us -> 39.9 us  [body(): pl.pallas_call(kernel, out_shape=jax.ShapeDtypeStruct((4, 128), F32), in_...]
where the time goes in v3:
time: 43.1 us; the launch traced here: 42.5 us
  Pallas kernels  39.9 us (93%)
  local copies, waits for them, and re-layouts  1.32 us (3%)
  between operations  1.29 us (3%)
    pallas_call x1, Pallas kernels, body(): pl.pallas_call(kernel, out_shape=jax.ShapeDtypeStruct((4, 128), F32), in_...  39.9 us
    slice x1, local copies, waits for them, and re-layouts, body(): return (out[0:2, :samples], out[2:4, :samples])  1.32 us

profile of v3, /device:TPU:1, one launch (start us, length us, event | category | flops | bytes accessed | tf_op | source)
XLA Modules:
  0.0 42.5 jit_solution(3312470910345571950)
XLA Ops:
  1.3 39.9 %shard_map.104 = f32[4,128]{1,0:T(4,128)} custom-call(s32[64,152]{1,0:T(8,128)} %occ_hbm.1, s32[1,64]{1,0:T(1,128)} %bitcast.5, s32[4,768]{1,0:T(4,128)} %orb_hbm.1, f32[2,768]{1,0:T(2,128)} %elem_hbm.1, s32[1,1]{1,0:T(1,128)} %bitcast.3.step_hbm, bf16[152,1024]{1,0:T(8,128)(2,1)} %w1_hbm.1, f32[1,1024]{1,0:T(1,128)} %bitcast.4, bf16[256,256]{1,0:T(8,128)(2,1)} %w2_hbm.1, ...), custom_call_target="tpu_custom_call" | custom-call | tf_op jit(solution)/shard_map/pallas_call | solution.py:522
  41.2 1.3 %fusion = (f32[2,64]{1,0:T(2,128)}, f32[2,64]{1,0:T(2,128)}) fusion(f32[4,128]{1,0:T(4,128)} %shard_map.104), kind=kLoop, calls=%fused_computation | loop fusion | bytes 2048 | tf_op jit(solution)/shard_map/slice | solution.py:553

commit v4 on v3

--- a/solution.py
+++ b/solution.py
@@ -92,6 +92,9 @@
     slot_hid,
     pick,
     pick_t,
+    hid_plane,
+    slope_plane,
+    kt_full,
     kt_hi,
     kt_lo,
     kr_hi,
@@ -102,8 +105,12 @@
     kp_buf,
     kl_msg,
     kl_buf,
+    yx_msg,
+    yx_buf,
     y_msg,
     y_buf,
+    zx_msg,
+    zx_buf,
     z_msg,
     z_buf,
     s_msg,
@@ -115,14 +122,20 @@
     op_recv,
     ol_send,
     ol_recv,
+    share_send,
+    share_recv,
     e_send,
     e_recv,
     kp_send,
     kp_recv,
     kl_send,
     kl_recv,
+    yx_send,
+    yx_recv,
     y_send,
     y_recv,
+    zx_send,
+    zx_recv,
     z_send,
     z_recv,
     s_send,
@@ -131,8 +144,6 @@
     outside = (occ_hbm, w2_hbm, w1_hbm, orb_hbm, counts_hbm, bias_hbm, elem_hbm, step_hbm, readout_hbm)
     inside = (occ_ref, w2_ref, w1_ref, orb_ref, counts_ref, bias_ref, elem_ref, step_ref, readout_ref)
     loads = [pltpu.make_async_copy(a, c, in_sem.at[i]) for i, (a, c) in enumerate(zip(outside, inside))]
-    for load in loads:
-        load.start()
     samples, orbitals = occ_ref.shape
     slots = orb_ref.shape[1]
     depth = w2_ref.shape[0]
@@ -173,10 +184,11 @@
             src_ref=src, dst_ref=dst, send_sem=send, recv_sem=recv, device_id=device, device_id_type=MESH
         )
 
-    def spread(peer, order, me, msg, buf, send, recv):
+    def spread(peer, order, me, msg, buf, send, recv, keep=True):
         for d in order:
             copy_to(msg, buf.at[me], send.at[d], recv.at[me], peer(d)[1]).start()
-        buf[me] = msg[...]
+        if keep:
+            buf[me] = msg[...]
 
     def collect(peer, order, msg, buf, send, recv):
         for d in order:
@@ -199,14 +211,24 @@
     for d in PLANE_ORDER:
         signal(plane_peer(d)[1])
 
-    def greet(d, carry):
-        signal(energy_peer(d))
-        return carry
-
-    lax.fori_loop(1, LINE * pn, greet, 0)
-
+    for dz in (0, *LINE_ORDER):
+        to_b = lax.rem(z + dz, LINE) * PLANE + w
+        for dp in range(pn):
+            if dz or dp:
+                signal((to_b, lax.rem(p + dp, pn)))
+    for load in loads:
+        load.start()
+
+    loads[0].wait()
+    occ = occ_ref[...].astype(F32)
+    occ_mine[...] = jnp.zeros_like(occ_mine)
+    core = p % 2
+    rows_here = samples // 2
+    for h in range(2):
+        occ_mine[h, :, :orbitals] = occ[h * rows_here : (h + 1) * rows_here].astype(BF16)
     pl.semaphore_wait(barrier, LINE * pn - 1 + PLANE - 1 + 1)
 
+    spread(*line, z, occ_mine.at[core], occ_line.at[core], ol_send, ol_recv, False)
     half = depth // 2
     whole = pl.ds(pl.multiple_of(p * depth, depth), depth)
     w2_copies = []
@@ -221,12 +243,9 @@
     for copy in w2_copies:
         copy.start()
 
-    loads[0].wait()
-    occ = occ_ref[...].astype(F32)
-    occ_mine[...] = jnp.zeros_like(occ_mine)
-    occ_mine[:, :orbitals] = occ.astype(BF16)
-    spread(*plane, w, occ_mine, occ_plane, op_send, op_recv)
-    spread(*line, z, occ_mine, occ_line, ol_send, ol_recv)
+    spread(*plane, w, occ_mine.at[core], occ_plane.at[core], op_send, op_recv, False)
+    occ_line[core, z] = occ_mine[core]
+    occ_plane[core, w] = occ_mine[core]
     loads[1].wait()
     w2_full[whole] = w2_ref[...]
 
@@ -259,11 +278,17 @@
             flip = flip | (orb[u : u + 1] == column)
         flipped = jnp.where(flip, 1.0 - base, base).astype(BF16)
         slot_hid[rows] = jnp.tanh(tn(flipped, w1) + bias).astype(BF16)
-    hidden = jnp.tanh(nn(occ_mine[:, :orbitals], w1) + bias).astype(BF16)
+    hidden = jnp.tanh(nn(occ.astype(BF16), w1) + bias).astype(BF16)
 
     for copy in w2_copies:
         copy.wait_recv()
     w2 = w2_full[...]
+    shares = [
+        copy_to(buf.at[core], buf.at[core], share_send.at[i], share_recv.at[i], (b, p_core))
+        for i, buf in enumerate((occ_line, occ_plane))
+    ]
+    collect(*line, occ_mine.at[core], occ_line.at[core], ol_send, ol_recv)
+    shares[0].start()
 
     readout = readout_ref[...]
     r_rows = pack_rows([x[i : i + 1] for x in parts3(readout) for i in range(2)], 128)
@@ -295,8 +320,7 @@
     e_rows = pack_rows([splits[i][j] for j in range(3) for i in range(2)], 16).astype(BF16)
     energy = nn(e_rows, pick[...])
     energy = energy[0:2] + energy[2:4] + energy[4:6]
-    e_msg[...] = jnp.zeros_like(e_msg)
-    e_msg[0:2, :samples] = energy
+    e_msg[...] = jnp.concatenate([energy, jnp.zeros((2, 128 - samples), F32)], axis=1)
 
     me = z * pn + p
 
@@ -309,21 +333,45 @@
                 e_copy(dz * pn + dp).start()
     e_buf[me] = e_msg[...]
 
-    collect(*plane, occ_mine, occ_plane, op_send, op_recv)
-    collect(*line, occ_mine, occ_line, ol_send, ol_recv)
-
-    def hidden_of(ref):
-        rows = ref[...].reshape(block, ref.shape[2])[:, :orbitals]
+    def fold(re, im):
+        return pack_rows([row[:, i * 128 : (i + 1) * 128] for row in (re, im) for i in range(block // 128)], 8)
+
+    def unfold(tile):
+        n = block // 128
+        return [jnp.concatenate([tile[at + i : at + i + 1] for i in range(n)], axis=1) for at in (0, n)]
+
+    def wide(row):
+        return jnp.concatenate([row] * (block // 128), axis=1)
+
+    def row_sum(value):
+        return jnp.broadcast_to(jnp.sum(value, axis=1, keepdims=True), (1, 128))
+
+    def hidden_of(parts):
+        rows = jnp.concatenate(parts, axis=0)[:, :orbitals]
         return jnp.tanh(nn(rows, w1) + bias).astype(BF16)
 
     def slope_of(hid):
         mid = jnp.tanh(nn(hid, w2))
         return 1.0 - mid * mid
 
-    hid_c = hidden_of(occ_line)
-    hid_r = hidden_of(occ_plane)
+    def half_of_plane(h):
+        hid = hidden_of([occ_plane[h, i] for i in range(PLANE)])
+        slope = slope_of(hid)
+        for i in range(PLANE):
+            rows = slice(i * rows_here, (i + 1) * rows_here)
+            hid_plane[i, h] = hid[rows]
+            slope_plane[i, h] = slope[rows]
+
+    collect(*plane, occ_mine.at[core], occ_plane.at[core], op_send, op_recv)
+    shares[1].start()
+    shares[0].wait_recv()
+    hid_c = hidden_of([occ_line[h, i] for i in range(LINE) for h in range(2)])
     slope_c = slope_of(hid_c)
-    slope_r = slope_of(hid_r)
+    half_of_plane(core)
+    shares[1].wait_recv()
+    half_of_plane(1 - core)
+    hid_r = hid_plane[...].reshape(block, hid_plane.shape[3])
+    slope_r = slope_plane[...].reshape(block, slope_plane.shape[3])
     gram = nt(hid_c, hid_r)
     r_hi = slope_r.astype(BF16)
     r_lo = (slope_r - r_hi.astype(F32)).astype(BF16)
@@ -338,16 +386,11 @@
         lo = (kt - hi.astype(F32)).astype(BF16)
         kt_hi[t] = hi
         kt_lo[t] = lo
+        kt_full[t] = kt
         ones_r.append(jnp.sum(kt, axis=0, keepdims=True))
-        turned = kt.T
-        hi = turned.astype(BF16)
-        kr_hi[t] = hi
-        kr_lo[t] = (turned - hi.astype(F32)).astype(BF16)
-        ones_c.append(jnp.sum(turned, axis=0, keepdims=True))
-    kp_msg[...] = pack_rows(ones_r, 8)
-    kl_msg[...] = pack_rows(ones_c, 8)
+    kp_msg[0:8] = fold(ones_r[0], ones_r[1])
+    kp_msg[8:16] = fold(ones_r[1], ones_r[2])
     spread(*plane, w, kp_msg, kp_buf, kp_send, kp_recv)
-    spread(*line, z, kl_msg, kl_buf, kl_send, kl_recv)
 
     def apply(va, vb, ones, k_hi, k_lo):
         ma = jnp.sum(va, axis=1, keepdims=True) * (1.0 / block)
@@ -371,15 +414,14 @@
         pairs = [tiles[i] + pltpu.roll(tiles[i + 1], samples, 1) for i in range(0, len(tiles), 2)]
         return jnp.concatenate(pairs, axis=1)
 
-    lane = lax.broadcasted_iota(jnp.int32, (8, 128), 1)
-
-    def piece(value, place):
-        for i in range(block // 128):
-            own_buf[i] = value[:, i * 128 : (i + 1) * 128]
-        tile = own_buf[place // 2]
-        odd = jnp.full(tile.shape, place % 2, jnp.int32) == 1
-        tile = jnp.where(odd, pltpu.roll(tile, samples, 1), tile)
-        return jnp.where(lane < samples, tile, 0.0)
+    lane = lax.broadcasted_iota(jnp.int32, (2, 128), 1)
+
+    def piece(tile, place):
+        own_buf[...] = tile
+        rows = jnp.concatenate([own_buf[pl.ds(place // 2, 1)], own_buf[pl.ds(place // 2 + 4, 1)]], axis=0)
+        odd = jnp.full(rows.shape, place % 2, jnp.int32) == 1
+        rows = jnp.where(odd, pltpu.roll(rows, samples, 1), rows)
+        return jnp.where(lane < samples, rows, 0.0)
 
     def e_wait(d, carry):
         to_b, to_p = energy_peer(d)
@@ -397,66 +439,82 @@
 
     energies = pieces([over_params(i) for i in range(LINE)])
     mine = over_params(z)
-    out_ref[0:2] = mine[0:2]
+    out_ref[0:2] = mine
 
     ea = energies[1:2] * (1.0 / total)
     eb = energies[0:1] * (-1.0 / total)
-    y_re, y_im = apply(ea, eb, ones_r, kt_hi, kt_lo)
-    y_msg[0:8] = pack_rows([y_re, y_im], 8)
-    y_msg[2:4, 0:128] = mine[0:2]
-    means = [jnp.sum(v, axis=1, keepdims=True) * (1.0 / total) for v in (ea, eb)]
-    y_msg[2:4, 128:256] = pack_rows([jnp.broadcast_to(v, (1, 128)) for v in means], 2)
+    yx_msg[0:2] = mine
+    yx_msg[2:3] = row_sum(ea) * (1.0 / total)
+    yx_msg[3:4] = row_sum(eb) * (1.0 / total)
+    spread(*plane, w, yx_msg, yx_buf, yx_send, yx_recv)
+    y_msg[...] = fold(*apply(ea, eb, ones_r, kt_hi, kt_lo))
     spread(*plane, w, y_msg, y_buf, y_send, y_recv)
+    for t in range(3):
+        turned = kt_full[t].T
+        hi = turned.astype(BF16)
+        kr_hi[t] = hi
+        kr_lo[t] = (turned - hi.astype(F32)).astype(BF16)
+        ones_c.append(jnp.sum(turned, axis=0, keepdims=True))
+    kl_msg[0:8] = fold(ones_c[0], ones_c[1])
+    kl_msg[8:16] = fold(ones_c[1], ones_c[2])
+    spread(*line, z, kl_msg, kl_buf, kl_send, kl_recv)
     collect(*plane, kp_msg, kp_buf, kp_send, kp_recv)
+    k1 = total_of(kp_buf)
+    collect(*plane, yx_msg, yx_buf, yx_send, yx_recv)
+    means = total_of(yx_buf)
+    ga, gb = means[2:3], means[3:4]
+    around = pieces([yx_buf[i] for i in range(PLANE)])
+    fa = around[1:2] * (1.0 / total) - wide(ga)
+    fb = around[0:1] * (-1.0 / total) - wide(gb)
+    fix = k1[0:8] * ga + k1[8:16] * gb
     collect(*plane, y_msg, y_buf, y_send, y_recv)
-    k1 = total_of(kp_buf)
-    y = total_of(y_buf)
-    ga, gb = y[2:3, 128:129], y[3:4, 128:129]
-    around = pieces([y_buf[i, :, 0:128] for i in range(PLANE)])
-    fa = around[3:4] * (1.0 / total) - ga
-    fb = around[2:3] * (-1.0 / total) - gb
-    f_re = y[0:1] - (k1[0:1] * ga + k1[1:2] * gb)
-    f_im = y[1:2] - (k1[1:2] * ga + k1[2:3] * gb)
-
+    f_tile = total_of(y_buf) - fix
+    f_re, f_im = unfold(f_tile)
+
+    f_mine = piece(f_tile, w)
+    zx_msg[0:2] = f_mine
+    zx_msg[2:3] = row_sum(f_re) * (1.0 / total)
+    zx_msg[3:4] = row_sum(f_im) * (1.0 / total)
+    zx_msg[4:5] = row_sum(fa * f_re + fb * f_im)
+    zx_msg[5:8] = jnp.zeros((3, 128), F32)
+    spread(*line, z, zx_msg, zx_buf, zx_send, zx_recv)
     ha = f_re * (1.0 / total) + DIAG_SHIFT * fa
     hb = f_im * (1.0 / total) + DIAG_SHIFT * fb
-    z_re, z_im = apply(ha, hb, ones_c, kr_hi, kr_lo)
-    z_msg[0:8] = pack_rows([z_re, z_im], 8)
-    f_mine = piece(pack_rows([f_re, f_im], 8), w)
-    z_msg[2:4, 0:128] = f_mine[0:2]
-    norm = jnp.sum(fa * f_re + fb * f_im, axis=1, keepdims=True)
-    means = [jnp.sum(v, axis=1, keepdims=True) * (1.0 / total) for v in (f_re, f_im)]
-    z_msg[2:5, 128:256] = pack_rows([jnp.broadcast_to(v, (1, 128)) for v in (*means, norm)], 3)
+    z_msg[...] = fold(*apply(ha, hb, ones_c, kr_hi, kr_lo))
     spread(*line, z, z_msg, z_buf, z_send, z_recv)
-    ca, cb = ea - ga, eb - gb
+    ca, cb = ea - wide(ga), eb - wide(gb)
     collect(*line, kl_msg, kl_buf, kl_send, kl_recv)
+    k1 = total_of(kl_buf)
+    collect(*line, zx_msg, zx_buf, zx_send, zx_recv)
+    acc = total_of(zx_buf)
+    f_mean, ff = acc[2:4], acc[4:5]
+    ga, gb = f_mean[0:1] * (1.0 / total), f_mean[1:2] * (1.0 / total)
+    fix = k1[0:8] * ga + k1[8:16] * gb
+    along = pieces([zx_buf[i, 0:2] for i in range(LINE)])
+    ha = along[0:1] * (1.0 / total) - wide(ga) + DIAG_SHIFT * ca
+    hb = along[1:2] * (1.0 / total) - wide(gb) + DIAG_SHIFT * cb
+    c_tile, h_tile = fold(ca, cb), fold(ha, hb)
     collect(*line, z_msg, z_buf, z_send, z_recv)
-    k1 = total_of(kl_buf)
-    acc = total_of(z_buf)
-    f_mean_re, f_mean_im, ff = acc[2:3, 128:129], acc[3:4, 128:129], acc[4:5, 128:129]
-    ga, gb = f_mean_re * (1.0 / total), f_mean_im * (1.0 / total)
-    a_re = acc[0:1] - (k1[0:1] * ga + k1[1:2] * gb)
-    a_im = acc[1:2] - (k1[1:2] * ga + k1[2:3] * gb)
-    along = pieces([z_buf[i, :, 0:128] for i in range(LINE)])
-    ha = along[2:3] * (1.0 / total) - ga + DIAG_SHIFT * ca
-    hb = along[3:4] * (1.0 / total) - gb + DIAG_SHIFT * cb
-
-    def inner(ua, ub, va, vb):
-        return jnp.sum(ua * va + ub * vb, axis=1, keepdims=True)
-
-    mean_re = jnp.sum(a_re, axis=1, keepdims=True) * (1.0 / block)
-    mean_im = jnp.sum(a_im, axis=1, keepdims=True) * (1.0 / block)
-    da, db = a_re - mean_re, a_im - mean_im
+    a_tile = total_of(z_buf) - fix
+
+    upper = lax.broadcasted_iota(jnp.int32, (8, 128), 0) < 4
+
+    def tile_sum(value):
+        return row_sum(jnp.sum(value, axis=0, keepdims=True))
+
+    mean_re = tile_sum(jnp.where(upper, a_tile, 0.0)) * (1.0 / block)
+    mean_im = tile_sum(jnp.where(upper, 0.0, a_tile)) * (1.0 / block)
+    apart = a_tile - jnp.where(upper, mean_re, mean_im)
     scalars = [
-        inner(ca, cb, a_re, a_im),
-        inner(ha, hb, a_re, a_im),
-        inner(da, db, da, db),
+        tile_sum(c_tile * a_tile),
+        tile_sum(h_tile * a_tile),
+        tile_sum(apart * apart),
         mean_re,
         mean_im,
     ]
-    s_msg[...] = pack_rows([jnp.broadcast_to(x, (1, 128)) for x in scalars], 8)
+    s_msg[...] = pack_rows(scalars, 8)
     spread(*plane, w, s_msg, s_buf, s_send, s_recv)
-    a_mine = piece(pack_rows([a_re, a_im], 8), z)
+    a_mine = piece(a_tile, z)
 
     for copy in w2_copies:
         copy.wait_send()
@@ -466,11 +524,15 @@
         return carry
 
     lax.fori_loop(1, LINE * pn, e_drain, 0)
-    drain(*plane, w, occ_mine, occ_plane, op_send, op_recv)
-    drain(*line, z, occ_mine, occ_line, ol_send, ol_recv)
+    drain(*plane, w, occ_mine.at[core], occ_plane.at[core], op_send, op_recv)
+    drain(*line, z, occ_mine.at[core], occ_line.at[core], ol_send, ol_recv)
+    for share in shares:
+        share.wait_send()
     drain(*plane, w, kp_msg, kp_buf, kp_send, kp_recv)
     drain(*line, z, kl_msg, kl_buf, kl_send, kl_recv)
+    drain(*plane, w, yx_msg, yx_buf, yx_send, yx_recv)
     drain(*plane, w, y_msg, y_buf, y_send, y_recv)
+    drain(*line, z, zx_msg, zx_buf, zx_send, zx_recv)
     drain(*line, z, z_msg, z_buf, z_send, z_recv)
 
     collect(*plane, s_msg, s_buf, s_send, s_recv)
@@ -479,8 +541,8 @@
     spread_sq = jnp.square(s_buf[0] - means)
     for j in range(1, PLANE):
         spread_sq = spread_sq + jnp.square(s_buf[j] - means)
-    f_af, af_af = s[0:1, 0:1], s[1:2, 0:1]
-    centered = s[2:3, 0:1] + float(block) * (spread_sq[3:4, 0:1] + spread_sq[4:5, 0:1])
+    f_af, af_af = s[0:1], s[1:2]
+    centered = s[2:3] + float(block) * (spread_sq[3:4] + spread_sq[4:5])
     af_aaf = centered * (1.0 / total) + DIAG_SHIFT * af_af
     alpha0 = ff / f_af
     rr = ff - 2.0 * alpha0 * f_af + alpha0 * alpha0 * af_af
@@ -490,8 +552,7 @@
     alpha1 = rr / curv
     on_f = alpha0 + alpha1 * near
     on_af = alpha1 * alpha0
-    out_ref[2:3] = on_f * (f_mine[0:1] - f_mean_re) - on_af * (a_mine[0:1] - means[3:4, 0:1])
-    out_ref[3:4] = on_f * (f_mine[1:2] - f_mean_im) - on_af * (a_mine[1:2] - means[4:5, 0:1])
+    out_ref[2:4] = on_f * (f_mine - f_mean) - on_af * (a_mine - means[3:5])
     drain(*plane, w, s_msg, s_buf, s_send, s_recv)
 
 
@@ -516,8 +577,8 @@
         readout,
     )
 
-    def message(n, width):
-        return [pltpu.VMEM((8, width), F32), pltpu.VMEM((n, 8, width), F32)]
+    def message(n, height):
+        return [pltpu.VMEM((height, 128), F32), pltpu.VMEM((n, height, 128), F32)]
 
     out = pl.pallas_call(
         kernel,
@@ -527,24 +588,29 @@
         scratch_shapes=[
             *[pltpu.VMEM(x.shape, x.dtype) for x in inputs],
             dma((9,)),
-            pltpu.VMEM((samples, 256), BF16),
-            pltpu.VMEM((LINE, samples, 256), BF16),
-            pltpu.VMEM((PLANE, samples, 256), BF16),
+            pltpu.VMEM((2, samples // 2, 256), BF16),
+            pltpu.VMEM((2, LINE, samples // 2, 256), BF16),
+            pltpu.VMEM((2, PLANE, samples // 2, 256), BF16),
             pltpu.VMEM((depth * PARAMS, hid2), BF16),
             pltpu.VMEM((slots, hid), BF16),
             pltpu.VMEM((slots, samples), BF16),
             pltpu.VMEM((samples, slots), BF16),
+            pltpu.VMEM((PLANE, 2, samples // 2, hid), BF16),
+            pltpu.VMEM((PLANE, 2, samples // 2, hid2), F32),
+            pltpu.VMEM((3, block, block), F32),
             *[pltpu.VMEM((3, block, block), BF16)] * 4,
-            *message(LINE * PARAMS, 128),
-            *message(PLANE, block),
-            *message(LINE, block),
-            *message(PLANE, block),
-            *message(LINE, block),
-            *message(PLANE, 128),
-            pltpu.VMEM((block // 128, 8, 128), F32),
+            *message(LINE * PARAMS, 2),
+            *message(PLANE, 16),
+            *message(LINE, 16),
+            *message(PLANE, 4),
+            *message(PLANE, 8),
+            *message(LINE, 8),
+            *message(LINE, 8),
+            *message(PLANE, 8),
+            pltpu.VMEM((8, 128), F32),
             dma((5,)),
             dma((5,)),
-            *[dma((n,)) for n in (8, 8, 8, 8, 32, 32, 8, 8, 8, 8, 8, 8, 8, 8, 8, 8)],
+            *[dma((n,)) for n in (8, 8, 8, 8, 2, 2, 32, 32, *[8] * 14)],
         ],
         compiler_params=pltpu.CompilerParams(
             collective_id=0, has_side_effects=True, vmem_limit_bytes=61 * 1024 * 1024

time: 43.1 us -> 41.6 us (0.965)
  Pallas kernels: 39.9 us -> 38.5 us
    pallas_call x1, Pallas kernels: 39.9 us -> 38.5 us  [body(): pl.pallas_call(kernel, out_shape=jax.ShapeDtypeStruct((4, 128), F32), in_...]
where the time goes in v4:
time: 41.6 us; the launch traced here: 41.1 us
  Pallas kernels  38.5 us (93%)
  local copies, waits for them, and re-layouts  1.32 us (3%)
  between operations  1.29 us (3%)
    pallas_call x1, Pallas kernels, body(): pl.pallas_call(kernel, out_shape=jax.ShapeDtypeStruct((4, 128), F32), in_...  38.5 us
    slice x1, local copies, waits for them, and re-layouts, body(): return (out[0:2, :samples], out[2:4, :samples])  1.32 us

profile of v4, /device:TPU:1, one launch (start us, length us, event | category | flops | bytes accessed | tf_op | source)
XLA Modules:
  0.0 41.1 jit_solution(5080677286088994942)
XLA Ops:
  1.3 38.5 %shard_map.104 = f32[4,128]{1,0:T(4,128)} custom-call(s32[64,152]{1,0:T(8,128)} %occ_hbm.1, s32[1,64]{1,0:T(1,128)} %bitcast.5, s32[4,768]{1,0:T(4,128)} %orb_hbm.1, f32[2,768]{1,0:T(2,128)} %elem_hbm.1, s32[1,1]{1,0:T(1,128)} %bitcast.3.step_hbm, bf16[152,1024]{1,0:T(8,128)(2,1)} %w1_hbm.1, f32[1,1024]{1,0:T(1,128)} %bitcast.4, bf16[256,256]{1,0:T(8,128)(2,1)} %w2_hbm.1, ...), custom_call_target="tpu_custom_call" | custom-call | tf_op jit(solution)/shard_map/pallas_call | solution.py:583
  39.8 1.3 %fusion = (f32[2,64]{1,0:T(2,128)}, f32[2,64]{1,0:T(2,128)}) fusion(f32[4,128]{1,0:T(4,128)} %shard_map.104), kind=kLoop, calls=%fused_computation | loop fusion | bytes 2048 | tf_op jit(solution)/shard_map/slice | solution.py:619

commit v5 on v4

--- a/solution.py
+++ b/solution.py
@@ -191,7 +191,7 @@
             buf[me] = msg[...]
 
     def collect(peer, order, msg, buf, send, recv):
-        for d in order:
+        for d in reversed(order):
             place, device = peer(d)
             copy_to(msg, buf.at[place], send.at[d], recv.at[place], device).wait_recv()
 
@@ -228,7 +228,6 @@
         occ_mine[h, :, :orbitals] = occ[h * rows_here : (h + 1) * rows_here].astype(BF16)
     pl.semaphore_wait(barrier, LINE * pn - 1 + PLANE - 1 + 1)
 
-    spread(*line, z, occ_mine.at[core], occ_line.at[core], ol_send, ol_recv, False)
     half = depth // 2
     whole = pl.ds(pl.multiple_of(p * depth, depth), depth)
     w2_copies = []
@@ -244,6 +243,7 @@
         copy.start()
 
     spread(*plane, w, occ_mine.at[core], occ_plane.at[core], op_send, op_recv, False)
+    spread(*line, z, occ_mine.at[core], occ_line.at[core], ol_send, ol_recv, False)
     occ_line[core, z] = occ_mine[core]
     occ_plane[core, w] = occ_mine[core]
     loads[1].wait()
@@ -280,6 +280,15 @@
         slot_hid[rows] = jnp.tanh(tn(flipped, w1) + bias).astype(BF16)
     hidden = jnp.tanh(nn(occ.astype(BF16), w1) + bias).astype(BF16)
 
+    readout = readout_ref[...]
+    r_rows = pack_rows([x[i : i + 1] for x in parts3(readout) for i in range(2)], 128)
+    r_cols = r_rows.T.astype(BF16)
+    angle = jnp.broadcast_to(step_ref[...].astype(F32), (1, slots)) * FIELD_RATE
+    field = FIELD_SCALE * sincos(angle)[0]
+    elem = elem_ref[...]
+    weight = elem[0:1] + field * elem[1:2]
+    slot_at = (p + pn * lax.broadcasted_iota(jnp.int32, (1, slots), 1)).astype(F32)
+    used = slot_at < ends[0:1, samples - 1 : samples]
     for copy in w2_copies:
         copy.wait_recv()
     w2 = w2_full[...]
@@ -290,10 +299,6 @@
     collect(*line, occ_mine.at[core], occ_line.at[core], ol_send, ol_recv)
     shares[0].start()
 
-    readout = readout_ref[...]
-    r_rows = pack_rows([x[i : i + 1] for x in parts3(readout) for i in range(2)], 128)
-    r_cols = r_rows.T.astype(BF16)
-
     def logs_of(hid):
         mid = jnp.tanh(nn(hid, w2))
         hi = mid.astype(BF16)
@@ -307,12 +312,6 @@
     parent_logs = nn(l_rows, pick_t[...])
     parent_logs = parent_logs[0:2] + parent_logs[2:4] + parent_logs[4:6]
     diff = slot_logs - parent_logs
-    angle = jnp.broadcast_to(step_ref[...].astype(F32), (1, slots)) * FIELD_RATE
-    field = FIELD_SCALE * sincos(angle)[0]
-    elem = elem_ref[...]
-    weight = elem[0:1] + field * elem[1:2]
-    slot_at = (p + pn * lax.broadcasted_iota(jnp.int32, (1, slots), 1)).astype(F32)
-    used = slot_at < ends[0:1, samples - 1 : samples]
     size = jnp.exp(diff[0:1])
     sin, cos = sincos(diff[1:2])
     contrib = [jnp.where(used, weight * (size * cos), 0.0), jnp.where(used, weight * (size * sin), 0.0)]
@@ -423,13 +422,16 @@
         rows = jnp.where(odd, pltpu.roll(rows, samples, 1), rows)
         return jnp.where(lane < samples, rows, 0.0)
 
-    def e_wait(d, carry):
-        to_b, to_p = energy_peer(d)
-        place = (to_b // PLANE) * pn + to_p
-        copy_to(e_msg, e_buf.at[place], e_send.at[d], e_recv.at[place], (to_b, to_p)).wait_recv()
-        return carry
-
-    lax.fori_loop(1, LINE * pn, e_wait, 0)
+    for dz in (0, *reversed(LINE_ORDER)):
+        to_z = lax.rem(z + dz, LINE)
+        for dp in range(pn):
+            if dz or dp:
+                to_p = lax.rem(p + dp, pn)
+                place = to_z * pn + to_p
+                d = dz * pn + dp
+                copy_to(
+                    e_msg, e_buf.at[place], e_send.at[d], e_recv.at[place], (to_z * PLANE + w, to_p)
+                ).wait_recv()
 
     def over_params(i):
         acc = e_buf[i * pn]

time: 41.6 us -> 41.5 us (level)
  no operation moved by 1% of the time
where the time goes in v5:
time: 41.5 us; the launch traced here: 40.9 us
  Pallas kernels  38.3 us (92%)
  local copies, waits for them, and re-layouts  1.32 us (3%)
  between operations  1.29 us (3%)
    pallas_call x1, Pallas kernels, body(): pl.pallas_call(kernel, out_shape=jax.ShapeDtypeStruct((4, 128), F32), in_...  38.3 us
    slice x1, local copies, waits for them, and re-layouts, body(): return (out[0:2, :samples], out[2:4, :samples])  1.32 us

profile of v5, /device:TPU:1, one launch (start us, length us, event | category | flops | bytes accessed | tf_op | source)
XLA Modules:
  0.0 40.9 jit_solution(11391261862814723659)
XLA Ops:
  1.3 38.3 %shard_map.104 = f32[4,128]{1,0:T(4,128)} custom-call(s32[64,152]{1,0:T(8,128)} %occ_hbm.1, s32[1,64]{1,0:T(1,128)} %bitcast.5, s32[4,768]{1,0:T(4,128)} %orb_hbm.1, f32[2,768]{1,0:T(2,128)} %elem_hbm.1, s32[1,1]{1,0:T(1,128)} %bitcast.3.step_hbm, bf16[152,1024]{1,0:T(8,128)(2,1)} %w1_hbm.1, f32[1,1024]{1,0:T(1,128)} %bitcast.4, bf16[256,256]{1,0:T(8,128)(2,1)} %w2_hbm.1, ...), custom_call_target="tpu_custom_call" | custom-call | tf_op jit(solution)/shard_map/pallas_call | solution.py:585
  39.6 1.3 %fusion = (f32[2,64]{1,0:T(2,128)}, f32[2,64]{1,0:T(2,128)}) fusion(f32[4,128]{1,0:T(4,128)} %shard_map.104), kind=kLoop, calls=%fused_computation | loop fusion | bytes 2048 | tf_op jit(solution)/shard_map/slice | solution.py:621
